TPU v7x, 512 devices: a whole 4x8x8 slice. The times are simulated.
512 devices in a mesh: seq: 32 (over z_hi, y, core), doc: 16 (over x, z_lo).
Axes of the slice: x: 4, y: 8, z: 8 (z_hi: 2, z_lo: 4; z = z_hi * 4 + z_lo), core: 2. Of those that a mesh axis runs over, the one named last changes fastest.
Arguments:
- self_q: bfloat16 [16, 4096, 4096], P('doc', 'seq'), may hold values from -5 to 5
- self_kv: bfloat16 [16, 4096, 2048], P('doc', 'seq'), may hold values from -5 to 5
- doc_ids: int32 [16, 4096], P('doc', 'seq'), may hold values from 0 to 7, never falling along the last dimension, each value on 1 to 1024 neighbouring positions
- cross_q: bfloat16 [16, 4096, 4096], P('doc', 'seq'), may hold values from -5 to 5
- vision_kv: bfloat16 [16, 32, 128, 2048], P(None, 'seq', 'doc'), may hold values from -5 to 5
- span_image: int32 [16, 64], P('doc'), may hold values from 0 to 31, as said below
- image_slot: int32 [16, 32], P('doc'), may hold values from 0 to 31, each once within a row
- cross_gate: float32 [1], replicated, may hold values from 0.5 to 1.5
Outputs:
- mixed: bfloat16 [16, 4096, 4096], P('doc', 'seq')
Inputs may be any that keep to these rules, and one draw needn't show every extreme that they name: `span_image`: non-decreasing along each document; every image 0 to 31 is attended by at least one span.
All inputs are finite; a program needn't handle non-finite values.
Results may differ from a plain program's by a relative error of at most 0.0075.
Values may be sent and summed in bfloat16 or wider, within the bound.
No kernel may reach another device: no remote copies, remote signals or barrier semaphores. Data moves between devices by JAX's collectives and lax.ppermute only.
A program may use at most 64 MiB of HBM per device.

v0:
```python
import jax
import jax.numpy as jnp
from jax import lax
from jax.sharding import PartitionSpec as P

HEADS = 32
KV_HEADS = 8
HEAD_DIM = 128


def split_heads(values):
    lead = values.shape[:-1]
    grouped = values.reshape(lead + (2, KV_HEADS, HEAD_DIM))
    grouped = jnp.moveaxis(grouped, -3, -2).reshape(lead + (KV_HEADS, 2 * HEAD_DIM))
    return jnp.repeat(grouped, HEADS // KV_HEADS, axis=-2)


def causal_attention(query, key, value, ids):
    length, heads_here = (query.shape[0], query.shape[1])
    block = min(512, length)
    scale = HEAD_DIM ** (-0.5)
    offsets = jnp.arange(block, dtype=jnp.int32)

    def query_step(index, result):
        q_start = index * block
        q_block = lax.dynamic_slice_in_dim(query, q_start, block, 0)
        q_ids = lax.dynamic_slice_in_dim(ids, q_start, block, 0)
        q_pos = q_start + offsets

        def key_step(inner, carry):
            running, total, accum = carry
            k_start = inner * block
            k_block = lax.dynamic_slice_in_dim(key, k_start, block, 0)
            v_block = lax.dynamic_slice_in_dim(value, k_start, block, 0)
            k_ids = lax.dynamic_slice_in_dim(ids, k_start, block, 0)
            k_pos = k_start + offsets
            visible = (k_pos[None, :] <= q_pos[:, None]) & (k_ids[None, :] == q_ids[:, None])
            scores = (
                jnp.einsum("qhd,khd->hqk", q_block, k_block, preferred_element_type=jnp.float32)
                * scale
            )
            scores = jnp.where(visible[None], scores, -1e30)
            newest = jnp.maximum(running, jnp.max(scores, axis=-1))
            weights = jnp.where(visible[None], jnp.exp(scores - newest[..., None]), 0.0)
            factor = jnp.exp(running - newest)
            total = total * factor + jnp.sum(weights, axis=-1)
            accum = accum * factor[..., None] + jnp.einsum(
                "hqk,khd->hqd",
                weights.astype(jnp.bfloat16),
                v_block,
                preferred_element_type=jnp.float32,
            )
            return (newest, total, accum)

        start_state = (
            jnp.full((heads_here, block), -1e30, jnp.float32),
            jnp.zeros((heads_here, block), jnp.float32),
            jnp.zeros((heads_here, block, HEAD_DIM), jnp.float32),
        )
        running, total, accum = lax.fori_loop(0, index + 1, key_step, start_state)
        context = (accum / total[..., None]).astype(jnp.bfloat16).transpose(1, 0, 2)
        return lax.dynamic_update_slice_in_dim(result, context, q_start, 0)

    return lax.fori_loop(0, length // block, query_step, jnp.zeros_like(query))


def cross_attention(cross_heads, images, span_ids, slots):
    length, heads_here = (cross_heads.shape[0], cross_heads.shape[1])
    image_count, vision_count = (images.shape[1], images.shape[2])
    span_count = span_ids.shape[0]
    span_len = length // span_count
    scale = HEAD_DIM ** (-0.5)
    image_range = jnp.arange(image_count, dtype=jnp.int32)
    slot = jnp.sum(jnp.where(span_ids[:, None] == image_range[None, :], slots[None, :], 0), axis=1)
    picker = (slot[:, None] == image_range[None, :]).astype(jnp.bfloat16)
    table = images.reshape(image_count, vision_count * heads_here * 2 * HEAD_DIM)
    chosen = jnp.dot(picker, table, preferred_element_type=jnp.float32).astype(jnp.bfloat16)
    chosen = chosen.reshape(span_count, vision_count, heads_here, 2 * HEAD_DIM)
    keys_here = chosen[..., :HEAD_DIM]
    values_here = chosen[..., HEAD_DIM:]
    queries = cross_heads.reshape(span_count, span_len, heads_here, HEAD_DIM)
    scores = (
        jnp.einsum("jthd,jvhd->jhtv", queries, keys_here, preferred_element_type=jnp.float32)
        * scale
    )
    top = jnp.max(scores, axis=-1, keepdims=True)
    weights = jnp.exp(scores - top)
    total = jnp.sum(weights, axis=-1)
    numer = jnp.einsum(
        "jhtv,jvhd->jthd",
        weights.astype(jnp.bfloat16),
        values_here,
        preferred_element_type=jnp.float32,
    )
    context = numer / total.transpose(0, 2, 1)[..., None]
    return context.astype(jnp.bfloat16).reshape(length, heads_here, HEAD_DIM)


def on_device(self_q, self_kv, doc_ids, cross_q, vision_kv, span_image, image_slot, cross_gate):
    tokens_here = self_q.shape[1]
    cross_heads = cross_q[0].reshape(tokens_here, HEADS, HEAD_DIM)
    images = lax.all_to_all(
        lax.all_to_all(split_heads(vision_kv), "seq", split_axis=3, concat_axis=1, tiled=True),
        "doc",
        split_axis=0,
        concat_axis=2,
        tiled=True,
    )
    q_heads = self_q[0].reshape(tokens_here, HEADS, HEAD_DIM)
    kv_heads = split_heads(self_kv[0])
    packed = jnp.concatenate([q_heads, kv_heads], axis=2)
    packed, cross_heads = (
        lax.all_to_all(packed, "seq", split_axis=1, concat_axis=0, tiled=True),
        lax.all_to_all(cross_heads, "seq", split_axis=1, concat_axis=0, tiled=True),
    )
    whole_ids = lax.all_gather(doc_ids, "seq", axis=1, tiled=True)[0]
    self_ctx = causal_attention(
        packed[..., :HEAD_DIM],
        packed[..., HEAD_DIM : 2 * HEAD_DIM],
        packed[..., 2 * HEAD_DIM :],
        whole_ids,
    )
    cross_ctx = cross_attention(cross_heads, images, span_image[0], image_slot[0])
    self_back, cross_back = (
        lax.all_to_all(self_ctx, "seq", split_axis=0, concat_axis=1, tiled=True),
        lax.all_to_all(cross_ctx, "seq", split_axis=0, concat_axis=1, tiled=True),
    )
    mixed = self_back.astype(jnp.float32) + jnp.tanh(cross_gate[0]) * cross_back.astype(jnp.float32)
    return mixed.astype(jnp.bfloat16).reshape(1, tokens_here, HEADS * HEAD_DIM)


def solution(mesh):
    in_specs = (
        P("doc", "seq", None),
        P("doc", "seq", None),
        P("doc", "seq"),
        P("doc", "seq", None),
        P(None, "seq", "doc", None),
        P("doc", None),
        P("doc", None),
        P(),
    )
    out_specs = P("doc", "seq", None)
    return jax.shard_map(
        on_device, mesh=mesh, in_specs=in_specs, out_specs=out_specs, check_vma=False
    )
```

profile of v0, /device:TPU:14, one launch (start us, length us, event | category | flops | bytes accessed | tf_op | source)
XLA Modules:
  0.0 539.4 jit_solution(6676314664974972805)
XLA Ops:
  1.3 1.6 broadcast_in_dim.52
  2.9 16.3 %all-to-all-start.2 = ((bf16[16,1,8,32,256]{4,2,0,1,3:T(8,128)(2,1)}), bf16[16,1,8,32,256]{4,2,0,1,3:T(8,128)(2,1)S(1)}, u32[]{:S(2)}, u32[]{:S(2)}) async-start(bf16[16,1,8,32,256]{4,2,0,1,3:T(8,128)(2,1)} %bitcast.24), calls=%async_computation.2 | async-start | bytes 4194304 | tf_op jit(solution)/shard_map/all_to_all | solution.py:103
  20.2 1.6 copy.56
  24.5 2.2 pad_maximum_fusion
  26.6 49.8 %all-to-all-done.2 = bf16[16,1,8,32,256]{4,2,0,1,3:T(8,128)(2,1)S(1)} async-done(((bf16[16,1,8,32,256]{4,2,0,1,3:T(8,128)(2,1)}), bf16[16,1,8,32,256]{4,2,0,1,3:T(8,128)(2,1)S(1)}, u32[]{:S(2)}, u32[]{:S(2)}) %all-to-all-start.2) | async-done | bytes 2097184 | tf_op jit(solution)/shard_map/all_to_all | solution.py:103
  77.7 7.1 %all-to-all-start = ((bf16[128,32,384]{2,0,1:T(8,128)(2,1)}), bf16[128,32,384]{2,0,1:T(8,128)(2,1)S(1)}, u32[]{:S(2)}, u32[]{:S(2)}) async-start(bf16[128,32,384]{2,0,1:T(8,128)(2,1)} %pad_maximum_fusion), calls=%async_computation | async-start | bytes 6291456 | tf_op jit(solution)/shard_map/all_to_all | solution.py:113
  87.7 76.1 %all-to-all-done = bf16[128,32,384]{2,0,1:T(8,128)(2,1)S(1)} async-done(((bf16[128,32,384]{2,0,1:T(8,128)(2,1)}), bf16[128,32,384]{2,0,1:T(8,128)(2,1)S(1)}, u32[]{:S(2)}, u32[]{:S(2)}) %all-to-all-start) | async-done | bytes 3145760 | tf_op jit(solution)/shard_map/all_to_all | solution.py:113
  163.7 18.4 %all-to-all-start.4 = ((bf16[128,32,128]{2,0,1:T(8,128)(2,1)}), bf16[128,32,128]{2,0,1:T(8,128)(2,1)}, u32[]{:S(2)}, u32[]{:S(2)}) async-start(bf16[128,32,128]{2,0,1:T(8,128)(2,1)} %copy.64), calls=%async_computation.4 | async-start | bytes 2097152 | tf_op jit(solution)/shard_map/all_to_all | solution.py:114
  182.2 68.6 %all_gather.3 = s32[1,4096]{1,0:T(1,128)} all-gather(s32[1,128]{1,0:T(1,128)S(1)} %copy-done.3), channel_id=1, replica_groups=mesh['seq'=32,'doc'=16] {'seq'}, dimensions={1}, use_global_device_ids=true | all-gather | bytes 16896 | tf_op jit(solution)/shard_map/all_gather | solution.py:116
  250.8 3.1 copy.62
  253.9 1.9 fusion.34
  255.8 6.6 %all-to-all-start.3 = ((bf16[16,32,8,1,256]{4,2,1,3,0:T(8,128)(2,1)}), bf16[16,32,8,1,256]{4,2,1,3,0:T(8,128)(2,1)S(1)}, u32[]{:S(2)}, u32[]{:S(2)}) async-start(bf16[16,32,8,1,256]{4,2,1,3,0:T(8,128)(2,1)} %copy.62), calls=%async_computation.3 | async-start | bytes 4194304 | tf_op jit(solution)/shard_map/all_to_all | solution.py:102
  262.5 186.8 %while.48 = (s32[]{:T(128)}, bf16[4096,1,128]{2,0,1:T(8,128)(2,1)S(1)}, s32[4096]{0:T(1024)}, bf16[4096,1,128]{2,0,1:T(8,128)(2,1)}, bf16[4096,1,128]{2,0,1:T(8,...) while((s32[]{:T(128)}, ...), condition=%wide.region_5.6_spmd.clone.clone, body=%wide.region_0.5_spmd.clone.clone.sunk | while | flops 139200512 | bytes 5061178 | solution.py:64
  264.9 4.6 while.49
  272.0 9.3 %while.49 = (s32[]{:T(128)}, f32[1,512]{1,0:T(1,128)S(1)}, f32[1,512]{1,0:T(1,128)S(1)}, f32[1,512,128]{2,1,0:T(8,128)S(1)}, s32[]{:T(128)}, /*index=5*/s32[512]...) while((s32[]{:T(128)}, f32[1,512]{1,0:T(1,128)S(1)}, ...), condition=%wide.region_4.4_spmd, body=%wide.region_1.3_spmd.sunk | while | flops 139068928 | bytes 4128979 | solution.py:60
  275.1 1.5 fusion.46
  283.8 13.9 %while.49 = (s32[]{:T(128)}, f32[1,512]{1,0:T(1,128)S(1)}, f32[1,512]{1,0:T(1,128)S(1)}, f32[1,512,128]{2,1,0:T(8,128)S(1)}, s32[]{:T(128)}, /*index=5*/s32[512]...) while((s32[]{:T(128)}, f32[1,512]{1,0:T(1,128)S(1)}, ...), condition=%wide.region_4.4_spmd, body=%wide.region_1.3_spmd.sunk | while | flops 139068928 | bytes 4128979 | solution.py:60
  300.2 18.5 %while.49 = (s32[]{:T(128)}, f32[1,512]{1,0:T(1,128)S(1)}, f32[1,512]{1,0:T(1,128)S(1)}, f32[1,512,128]{2,1,0:T(8,128)S(1)}, s32[]{:T(128)}, /*index=5*/s32[512]...) while((s32[]{:T(128)}, f32[1,512]{1,0:T(1,128)S(1)}, ...), condition=%wide.region_4.4_spmd, body=%wide.region_1.3_spmd.sunk | while | flops 139068928 | bytes 4128979 | solution.py:60
  317.2 1.5 fusion.46
  321.3 23.2 %while.49 = (s32[]{:T(128)}, f32[1,512]{1,0:T(1,128)S(1)}, f32[1,512]{1,0:T(1,128)S(1)}, f32[1,512,128]{2,1,0:T(8,128)S(1)}, s32[]{:T(128)}, /*index=5*/s32[512]...) while((s32[]{:T(128)}, f32[1,512]{1,0:T(1,128)S(1)}, ...), condition=%wide.region_4.4_spmd, body=%wide.region_1.3_spmd.sunk | while | flops 139068928 | bytes 4128979 | solution.py:60
  333.7 1.5 fusion.46
  338.3 1.5 fusion.46
  342.9 1.5 fusion.46
  346.9 27.8 %while.49 = (s32[]{:T(128)}, f32[1,512]{1,0:T(1,128)S(1)}, f32[1,512]{1,0:T(1,128)S(1)}, f32[1,512,128]{2,1,0:T(8,128)S(1)}, s32[]{:T(128)}, /*index=5*/s32[512]...) while((s32[]{:T(128)}, f32[1,512]{1,0:T(1,128)S(1)}, ...), condition=%wide.region_4.4_spmd, body=%wide.region_1.3_spmd.sunk | while | flops 139068928 | bytes 4128979 | solution.py:60
  364.0 1.5 fusion.46
  368.6 1.5 fusion.46
  373.2 1.5 fusion.46
  377.2 32.4 %while.49 = (s32[]{:T(128)}, f32[1,512]{1,0:T(1,128)S(1)}, f32[1,512]{1,0:T(1,128)S(1)}, f32[1,512,128]{2,1,0:T(8,128)S(1)}, s32[]{:T(128)}, /*index=5*/s32[512]...) while((s32[]{:T(128)}, f32[1,512]{1,0:T(1,128)S(1)}, ...), condition=%wide.region_4.4_spmd, body=%wide.region_1.3_spmd.sunk | while | flops 139068928 | bytes 4128979 | solution.py:60
  394.3 1.5 fusion.46
  398.9 1.5 fusion.46
  403.5 1.5 fusion.46
  408.1 1.5 fusion.46
  412.2 37.0 %while.49 = (s32[]{:T(128)}, f32[1,512]{1,0:T(1,128)S(1)}, f32[1,512]{1,0:T(1,128)S(1)}, f32[1,512,128]{2,1,0:T(8,128)S(1)}, s32[]{:T(128)}, /*index=5*/s32[512]...) while((s32[]{:T(128)}, f32[1,512]{1,0:T(1,128)S(1)}, ...), condition=%wide.region_4.4_spmd, body=%wide.region_1.3_spmd.sunk | while | flops 139068928 | bytes 4128979 | solution.py:60
  415.3 1.5 fusion.46
  424.5 1.5 fusion.46
  438.4 1.5 fusion.46
  447.7 1.5 fusion.46
  449.9 2.0 reduce.9
  451.9 2.2 reshape.155
  454.0 5.6 %all-to-all-start.1 = ((bf16[32,2,8192]{2,1,0:T(2,128)(2,1)}), bf16[32,2,8192]{2,1,0:T(2,128)(2,1)S(1)}, u32[]{:S(2)}, u32[]{:S(2)}) async-start(bf16[32,2,8192]{2,1,0:T(2,128)(2,1)} %reshape.155), calls=%async_computation.1 | async-start | bytes 2097152 | tf_op jit(solution)/shard_map/all_to_all | solution.py:125
  459.7 1.6 copy.63
  461.3 2.9 reshape.144
  466.6 2.9 bitcast_reduce_fusion
  474.7 18.1 %all-to-all-done.1 = bf16[32,2,8192]{2,1,0:T(2,128)(2,1)S(1)} async-done(((bf16[32,2,8192]{2,1,0:T(2,128)(2,1)}), bf16[32,2,8192]{2,1,0:T(2,128)(2,1)S(1)}, u32[]{:S(2)}, u32[]{:S(2)}) %all-to-all-start.1) | async-done | bytes 1048608 | tf_op jit(solution)/shard_map/all_to_all | solution.py:125
  492.8 4.4 all-to-all-start.5
  499.0 30.8 %all-to-all-done.5 = bf16[32,2,8192]{2,1,0:T(2,128)(2,1)} async-done(((bf16[32,2,8192]{2,1,0:T(2,128)(2,1)}), bf16[32,2,8192]{2,1,0:T(2,128)(2,1)}, u32[]{:S(2)}, u32[]{:S(2)}) %all-to-all-start.5) | async-done | bytes 1048608 | tf_op jit(solution)/shard_map/all_to_all | solution.py:126
  529.8 5.8 %reshape.154 = bf16[4096,1,128]{2,1,0:T(2,128)(2,1)} reshape(bf16[32,2,8192]{2,1,0:T(2,128)(2,1)} %all-to-all-done.5) | data formatting | bytes 2097152
  535.6 1.9 add_convert_fusion
  (370 shorter events, 180.9 us)
Async XLA Ops:
  2.9 16.3 %copy-start.2 = (bf16[1,128,2048]{2,1,0:T(8,128)(2,1)S(1)}, bf16[1,128,2048]{2,1,0:T(8,128)(2,1)}, u32[]{:S(2)}) copy-start(bf16[1,128,2048]{2,1,0:T(8,128)(2,1)} %param.13) | copy-start | bytes 1572868
  2.9 73.5 %all-to-all-start.2 = ((bf16[16,1,8,32,256]{4,2,0,1,3:T(8,128)(2,1)}), bf16[16,1,8,32,256]{4,2,0,1,3:T(8,128)(2,1)S(1)}, u32[]{:S(2)}, u32[]{:S(2)}) async-start(bf16[16,1,8,32,256]{4,2,0,1,3:T(8,128)(2,1)} %bitcast.24), calls=%async_computation.2 | async-start | bytes 4194304 | tf_op jit(solution)/shard_map/all_to_all | solution.py:103
  23.1 1.4 copy-start.1
  76.4 1.4 copy-start
  77.7 86.0 %all-to-all-start = ((bf16[128,32,384]{2,0,1:T(8,128)(2,1)}), bf16[128,32,384]{2,0,1:T(8,128)(2,1)S(1)}, u32[]{:S(2)}, u32[]{:S(2)}) async-start(bf16[128,32,384]{2,0,1:T(8,128)(2,1)} %pad_maximum_fusion), calls=%async_computation | async-start | bytes 6291456 | tf_op jit(solution)/shard_map/all_to_all | solution.py:113
  86.3 95.9 %copy-start.3 = (s32[1,128]{1,0:T(1,128)S(1)}, s32[1,128]{1,0:T(1,128)}, u32[]{:S(2)}) copy-start(s32[1,128]{1,0:T(1,128)} %param.14) | copy-start | bytes 1540
  163.7 92.1 %all-to-all-start.4 = ((bf16[128,32,128]{2,0,1:T(8,128)(2,1)}), bf16[128,32,128]{2,0,1:T(8,128)(2,1)}, u32[]{:S(2)}, u32[]{:S(2)}) async-start(bf16[128,32,128]{2,0,1:T(8,128)(2,1)} %copy.64), calls=%async_computation.4 | async-start | bytes 2097152 | tf_op jit(solution)/shard_map/all_to_all | solution.py:114
  255.8 198.2 %all-to-all-start.3 = ((bf16[16,32,8,1,256]{4,2,1,3,0:T(8,128)(2,1)}), bf16[16,32,8,1,256]{4,2,1,3,0:T(8,128)(2,1)S(1)}, u32[]{:S(2)}, u32[]{:S(2)}) async-start(bf16[16,32,8,1,256]{4,2,1,3,0:T(8,128)(2,1)} %copy.62), calls=%async_computation.3 | async-start | bytes 4194304 | tf_op jit(solution)/shard_map/all_to_all | solution.py:102
  451.9 7.7 %copy-start.4 = (s32[1,32]{1,0:T(1,128)S(1)}, s32[1,32]{1,0:T(1,128)}, u32[]{:S(2)}) copy-start(s32[1,32]{1,0:T(1,128)} %param.18) | copy-start | bytes 388
  451.9 7.8 %copy-start.5 = (s32[1,64]{1,0:T(1,128)S(1)}, s32[1,64]{1,0:T(1,128)}, u32[]{:S(2)}) copy-start(s32[1,64]{1,0:T(1,128)} %param.17) | copy-start | bytes 772
  454.0 38.8 %all-to-all-start.1 = ((bf16[32,2,8192]{2,1,0:T(2,128)(2,1)}), bf16[32,2,8192]{2,1,0:T(2,128)(2,1)S(1)}, u32[]{:S(2)}, u32[]{:S(2)}) async-start(bf16[32,2,8192]{2,1,0:T(2,128)(2,1)} %reshape.155), calls=%async_computation.1 | async-start | bytes 2097152 | tf_op jit(solution)/shard_map/all_to_all | solution.py:125
  492.8 37.0 %all-to-all-start.5 = ((bf16[32,2,8192]{2,1,0:T(2,128)(2,1)}), bf16[32,2,8192]{2,1,0:T(2,128)(2,1)}, u32[]{:S(2)}, u32[]{:S(2)}) async-start(bf16[32,2,8192]{2,1,0:T(2,128)(2,1)} %reshape.153), calls=%async_computation.5 | async-start | bytes 2097152 | tf_op jit(solution)/shard_map/all_to_all | solution.py:126
where the time goes:
time: 544 us; the launch traced here: 539 us
  waiting for transfers between devices  175 us (32%)
  matrix products  106 us (19%)
  local copies, waits for them, and re-layouts  81.2 us (15%)
  blocking collectives  68.6 us (13%)
  starting transfers between devices  58.4 us (11%)
  other arithmetic  47.1 us (9%)
    all_to_all x1, waiting for transfers between devices, on_device(): lax.all_to_all(packed, 'seq', split_axis=1, concat_axis=0, tiled=True)  76.1 us
    all_gather x1, blocking collectives, on_device(): whole_ids = lax.all_gather(doc_ids, 'seq', axis=1, tiled=True)[0]  68.6 us
    dot_general x36, matrix products, key_step(): jnp.einsum('hqk,khd->hqd', weights.astype(jnp.bfloat16), v_block, preferr...  53.9 us
    all_to_all x1, waiting for transfers between devices, on_device(): lax.all_to_all(split_heads(vision_kv), 'seq', split_axis=3, concat_axis=1...  49.8 us
    dot_general x36, matrix products, key_step(): jnp.einsum('qhd,khd->hqk', q_block, k_block, preferred_element_type=jnp.f...  46.5 us
    all_to_all x1, waiting for transfers between devices, on_device(): lax.all_to_all(cross_ctx, 'seq', split_axis=0, concat_axis=1, tiled=True)  30.8 us
    dynamic_slice x36, local copies, waits for them, and re-layouts, key_step(): k_ids = lax.dynamic_slice_in_dim(ids, k_start, block, 0)  27.3 us
    add x36, other arithmetic, key_step(): k_pos = k_start + offsets  24.6 us
  transfers between devices with their start and end apart: 6, of which 4 were waited for; matrix products, arithmetic and copies ran while one was open for 41% of the time, Pallas kernels for 0%

commit v1 on v0

v1 whole, which is shorter than its diff:
```python
import math

import jax
import jax.numpy as jnp
from jax import lax
from jax.experimental import pallas as pl
from jax.experimental.pallas import tpu as pltpu
from jax.sharding import Mesh, PartitionSpec as P

HEADS = 32
KV_HEADS = 8
DIM = 128
GROUP = HEADS // KV_HEADS
HOPS = 4
ID_ROWS = 16
VMEM = 62 * 2**20
NEG = -1e30
EXP2_SCALE = DIM ** -0.5 * math.log2(math.e)

ROWS, LINE, CORES = 2, 8, 2
AXES = ("zh", "y", "core", "x", "zl")
SEQ = ("zh", "y", "core")
DOC = ("x", "zl")


def place(zh, y, core):
    return (zh * LINE + y) * CORES + core


def pairs(moves):
    return [(place(*a, c), place(*b, c)) for a, b in moves for c in range(CORES)]


SWAP = [(place(z, y, c), place(z, y, 1 - c)) for z in range(ROWS) for y in range(LINE) for c in range(CORES)]


CROSS = pairs([((0, LINE - HOPS + j), (1, j)) for j in range(HOPS)])
LAST = pairs([((0, LINE - 1), (1, 0))])


def back_step(step):
    return pairs([((1, j + 1), (1, j)) for j in range(HOPS - step)])


def move(value, perm):
    return lax.ppermute(value, SEQ, perm)


def self_kernel(place_ref, q_own_ref, q_far_ref, *refs):
    count = 2 * HOPS + 1
    keys, values, ids = refs[:count], refs[count : 2 * count], refs[2 * count : 3 * count]
    out_own_ref, out_far_ref, bias_ref = refs[3 * count :]
    span = keys[0].shape[0]
    row, y, core = place_ref[0], place_ref[1], place_ref[2]

    def window(parts, take):
        blocks = [take(parts[0][...])]
        for hop in range(1, HOPS + 1):
            blocks.append(jnp.where(y >= hop, take(parts[hop][0]), take(parts[HOPS + hop][...])))
        return blocks

    @pl.when(pl.program_id(0) == 0)
    def _():
        numbers = window(ids, lambda block: jnp.broadcast_to(block[0:1].astype(jnp.float32), (span, span)))
        of_query = numbers[0].T
        own_half = core * (span // CORES)
        q_at = lax.broadcasted_iota(jnp.int32, (span, span), 0) ^ own_half
        k_at = lax.broadcasted_iota(jnp.int32, (span, span), 1) ^ own_half
        for hop in range(HOPS + 1):
            seen = numbers[hop] == of_query
            if hop == 0:
                seen = seen & (k_at <= q_at)
            else:
                seen = seen & ((row > 0) | (y >= hop))
            bias_ref[:, hop * span : (hop + 1) * span] = jnp.where(seen, 0.0, NEG)

    key = jnp.concatenate(window(keys, lambda block: block), 0)
    value = jnp.concatenate(window(values, lambda block: block), 0)
    rows = q_own_ref.shape[0]
    for h in range(GROUP):
        cols = slice(h * DIM, (h + 1) * DIM)
        query = jnp.concatenate([q_own_ref[:, cols], q_far_ref[:, cols]], 0)
        s = lax.dot_general(query, key, (((1,), (1,)), ((), ())), preferred_element_type=jnp.float32)
        s = s + bias_ref[...]
        top = jnp.max(s, axis=1, keepdims=True)
        w = jnp.exp2((s - top) * EXP2_SCALE)
        den = jnp.sum(w, axis=1, keepdims=True)
        num = jnp.dot(w.astype(jnp.bfloat16), value, preferred_element_type=jnp.float32)
        ctx = (num / den).astype(jnp.bfloat16)
        out_own_ref[:, cols] = ctx[:rows]
        out_far_ref[:, cols] = ctx[rows:]


def self_attention(place, q_own, q_far, own, line, across):
    tokens, width = q_own.shape
    span = CORES * tokens
    half = KV_HEADS // CORES
    window = (HOPS + 1) * span
    q_spec = pl.BlockSpec((tokens, GROUP * DIM), lambda g, at: (0, g))

    def specs(shape, index):
        before = [lambda g, at, hop=hop: (jnp.maximum(at[1] - hop, 0),) + index(g) for hop in range(1, HOPS + 1)]
        plain = pl.BlockSpec(shape, lambda g, at: index(g))
        return [plain] + [pl.BlockSpec((1,) + shape, f) for f in before] + [plain] * HOPS

    return pl.pallas_call(
        self_kernel,
        grid_spec=pltpu.PrefetchScalarGridSpec(
            num_scalar_prefetch=1,
            grid=(half,),
            in_specs=[q_spec, q_spec]
            + specs((span, DIM), lambda g: (0, g))
            + specs((span, DIM), lambda g: (0, half + g))
            + specs((ID_ROWS, span), lambda g: (span // ID_ROWS, 0)),
            out_specs=[q_spec, q_spec],
            scratch_shapes=[pltpu.VMEM((span, window), jnp.float32)],
        ),
        out_shape=[jax.ShapeDtypeStruct((tokens, width), jnp.bfloat16)] * 2,
        compiler_params=pltpu.CompilerParams(vmem_limit_bytes=VMEM),
        cost_estimate=pl.CostEstimate(
            flops=4 * span * window * width, bytes_accessed=8 * 2**20, transcendentals=span * window * width // DIM
        ),
        name="self_attention",
    )(place, q_own, q_far, *([own] + [line] * HOPS + across) * 3)


def pick_kernel(rows_ref, places_ref, table_ref, out_ref):
    for i in range(out_ref.shape[0]):
        out_ref[i] = table_ref[rows_ref[i], :, places_ref[i]]


def pick(slots, table):
    places = table.shape[2]
    smem, vmem = pl.BlockSpec(memory_space=pltpu.SMEM), pl.BlockSpec(memory_space=pltpu.VMEM)
    return pl.pallas_call(
        pick_kernel,
        in_specs=[smem, smem, vmem],
        out_specs=vmem,
        out_shape=jax.ShapeDtypeStruct(slots.shape + (table.shape[1],) + table.shape[3:], table.dtype),
        cost_estimate=pl.CostEstimate(flops=0, bytes_accessed=4 * table.size, transcendentals=0),
        compiler_params=pltpu.CompilerParams(vmem_limit_bytes=VMEM),
        name="pick_images",
    )(slots // places, slots % places, table)


def cross_kernel(core_ref, gate_ref, q_ref, key_ref, value_ref, own_ref, far_ref, out_ref):
    here = (pl.program_id(0) // (KV_HEADS // CORES)) == core_ref[0]
    gate = gate_ref[0]
    spans = key_ref.shape[1]
    span = q_ref.shape[0] // spans
    for j in range(spans):
        rows = slice(j * span, (j + 1) * span)
        q = jnp.concatenate([q_ref[rows, h * DIM : (h + 1) * DIM] for h in range(GROUP)], 0)
        s = lax.dot_general(q, key_ref[0, j], (((1,), (1,)), ((), ())), preferred_element_type=jnp.float32)
        top = jnp.max(s, axis=1, keepdims=True)
        w = jnp.exp2((s - top) * EXP2_SCALE)
        den = jnp.sum(w, axis=1, keepdims=True)
        num = jnp.dot(w.astype(jnp.bfloat16), value_ref[0, j], preferred_element_type=jnp.float32)
        cross = (num / den).astype(jnp.bfloat16).astype(jnp.float32)
        for h in range(GROUP):
            cols = slice(h * DIM, (h + 1) * DIM)
            own, far = own_ref[rows, cols].astype(jnp.float32), far_ref[rows, cols].astype(jnp.float32)
            mixed = jnp.where(here, own, far) + gate * cross[h * span : (h + 1) * span]
            out_ref[rows, cols] = mixed.astype(jnp.bfloat16)


def cross_attention(core, gate, cross_q, images, own, far):
    tokens, width = cross_q.shape
    half = KV_HEADS // CORES
    smem = pl.BlockSpec(memory_space=pltpu.SMEM)
    q_spec = pl.BlockSpec((tokens, GROUP * DIM), lambda g: (0, g))
    half_spec = pl.BlockSpec((tokens, GROUP * DIM), lambda g: (0, g % half))
    image = (1,) + images.shape[1:]
    return pl.pallas_call(
        cross_kernel,
        grid=(KV_HEADS,),
        in_specs=[
            smem,
            smem,
            q_spec,
            pl.BlockSpec(image, lambda g: (g, 0, 0, 0)),
            pl.BlockSpec(image, lambda g: (KV_HEADS + g, 0, 0, 0)),
            half_spec,
            half_spec,
        ],
        out_specs=q_spec,
        out_shape=jax.ShapeDtypeStruct((tokens, width), jnp.bfloat16),
        cost_estimate=pl.CostEstimate(
            flops=4 * tokens * images.shape[2] * width,
            bytes_accessed=6 * 2**20,
            transcendentals=tokens * images.shape[2] * HEADS,
        ),
        compiler_params=pltpu.CompilerParams(vmem_limit_bytes=VMEM),
        name="cross_attention",
    )(core, gate, cross_q, images, images, own, far)


def on_device(self_q, self_kv, doc_ids, cross_q, vision_kv, span_image, image_slot, cross_gate):
    q, kv, cq = self_q[0], self_kv[0], cross_q[0]
    tokens = q.shape[0]
    core = lax.axis_index("core")
    first = core == 0

    def halves(value):
        lo, hi = jnp.split(value, 2, axis=1)
        return jnp.where(first, lo, hi), jnp.where(first, hi, lo)

    k_mine, k_other = halves(kv[:, : KV_HEADS * DIM])
    v_mine, v_other = halves(kv[:, KV_HEADS * DIM :])
    numbers = (doc_ids + 1).astype(jnp.bfloat16)
    width = KV_HEADS * DIM
    numbers_own = jnp.pad(numbers, ((0, ID_ROWS - 1), (0, width - tokens)))
    numbers_far = jnp.pad(numbers, ((0, ID_ROWS - 1), (tokens, width - 2 * tokens)))
    far = move(jnp.concatenate([jnp.concatenate([k_other, v_other], 1), numbers_far], 0), SWAP)
    own = jnp.concatenate([jnp.concatenate([k_mine, v_mine], 1), far[:tokens], numbers_own + far[tokens:]], 0)

    docs, chunk = vision_kv.shape[0], vision_kv.shape[2]
    places = LINE * CORES
    image = vision_kv[:, 0].reshape(docs, chunk, places, DIM).transpose(2, 0, 1, 3)
    spread = lax.all_to_all(image, ("y", "core"), 0, 0, tiled=True)

    back0 = move(own, CROSS)
    last = move(own, LAST)
    gathered, spread = lax.optimization_barrier((own, spread))
    line = lax.all_gather(gathered, "y", axis=0)
    spread = spread.transpose(1, 0, 2, 3)
    table = lax.all_to_all(jnp.concatenate([spread, spread], 0), ("zh",) + DOC, 0, 0, tiled=True)
    table = table.reshape(ROWS, docs, places, chunk, DIM)
    back1 = move(back0, back_step(1))
    back2 = move(back1, back_step(2))
    q_own, q_other = halves(q)
    q_far = move(q_other, SWAP)
    image_range = jnp.arange(image_slot.shape[1], dtype=jnp.int32)
    slot = jnp.sum(jnp.where(span_image[0][:, None] == image_range[None, :], image_slot[0][None, :], 0), axis=1)
    here = slot.reshape(ROWS, -1)
    here = jnp.where(lax.axis_index("zh") == 0, here[0], here[1])
    table, _, _ = lax.optimization_barrier((table, back2, last))
    chosen = pick(here, table)
    chosen = chosen.reshape((places, -1) + chosen.shape[1:])
    images = lax.all_to_all(chosen, ("y", "core"), 0, 0, tiled=True)
    images = images.reshape(images.shape[:2] + (-1, DIM))

    place = jnp.stack([lax.axis_index("zh"), lax.axis_index("y"), core]).astype(jnp.int32)
    ctx_own, ctx_other = self_attention(place, q_own, q_far, own, line, [last, back2, back1, back0])
    ctx_far = move(ctx_other, SWAP)
    mixed = cross_attention(place[2:], jnp.tanh(cross_gate), cq, images, ctx_own, ctx_far)
    return mixed[None]


def solution(mesh):
    split = Mesh(mesh.devices.reshape(ROWS, LINE, CORES, 4, 4), AXES)
    in_specs = (
        P(DOC, SEQ, None),
        P(DOC, SEQ, None),
        P(DOC, SEQ),
        P(DOC, SEQ, None),
        P(None, SEQ, DOC, None),
        P(DOC, None),
        P(DOC, None),
        P(),
    )
    return jax.shard_map(on_device, mesh=split, in_specs=in_specs, out_specs=P(DOC, SEQ, None), check_vma=False)
```

time: 544 us -> 174 us (0.32)
  the two profiles are of different devices: /device:TPU:14 before, /device:TPU:257 now
where the time goes in v1:
time: 174 us; the launch traced here: 173 us
  waiting for transfers between devices  88.4 us (51%)
  starting transfers between devices  35.5 us (20%)
  Pallas kernels  25 us (14%)
  between operations  14.3 us (8%)
  local copies, waits for them, and re-layouts  5.37 us (3%)
  other arithmetic  4.02 us (2%)
    ppermute x7, waiting for transfers between devices, move(): return lax.ppermute(value, SEQ, perm)  70.5 us
    pallas_call x1, Pallas kernels, self_attention(): pl.pallas_call(self_kernel, grid_spec=pltpu.PrefetchScalarGridSpec(num_sc...  14.1 us
    all_to_all x1, waiting for transfers between devices, on_device(): spread = lax.all_to_all(image, ('y', 'core'), 0, 0, tiled=True)  12.8 us
    ppermute x7, starting transfers between devices, move(): return lax.ppermute(value, SEQ, perm)  11.4 us
    all_to_all x1, starting transfers between devices, on_device(): lax.all_to_all(jnp.concatenate([spread, spread], 0), ('zh',) + DOC, 0, 0,...  9.49 us
    pallas_call x1, Pallas kernels, cross_attention(): pl.pallas_call(cross_kernel, grid=(KV_HEADS,), in_specs=[smem, smem, q_sp...  8.44 us
    all_to_all x1, starting transfers between devices, on_device(): spread = lax.all_to_all(image, ('y', 'core'), 0, 0, tiled=True)  7.92 us
    all_to_all x1, starting transfers between devices, on_device(): images = lax.all_to_all(chosen, ('y', 'core'), 0, 0, tiled=True)  6.66 us
  transfers between devices with their start and end apart: 11, of which 8 were waited for; matrix products, arithmetic and copies ran while one was open for 3% of the time, Pallas kernels for 10%

profile of v1, /device:TPU:257, one launch (start us, length us, event | category | flops | bytes accessed | tf_op | source)
XLA Modules:
  0.0 172.7 jit_solution(2972220082486397995)
XLA Ops:
  6.5 1.1 copy.18
  7.7 0.0 copy-start.7
  7.7 0.9 copy.14
  8.6 7.9 %all-to-all-start = ((bf16[16,16,8,128]{3,2,1,0:T(8,128)(2,1)}), bf16[16,16,8,128]{3,2,1,0:T(8,128)(2,1)S(1)}, u32[]{:S(2)}, u32[]{:S(2)}) async-start(bf16[16,16,8,128]{3,2,1,0:T(8,128)(2,1)} %copy.14), calls=%async_computation | async-start | bytes 1048576 | tf_op jit(solution)/shard_map/all_to_all | solution.py:220
  16.6 0.0 all-gather.3.cloned.1.call-start
  16.6 0.0 copy-done.7
  16.7 0.0 copy-done.9
  16.7 2.0 %collective-permute-start = (bf16[144,1024]{1,0:T(8,128)(2,1)S(1)}, bf16[144,1024]{1,0:T(8,128)(2,1)S(1)}, u32[]{:S(2)}, u32[]{:S(2)}) collective-permute-start(bf16[144,1024]{1,0:T(8,128)(2,1)S(1)} %fusion.1), channel_id=1, source_target_pairs={{0,16},{16,0},{32,48},{48,32},{64,80},{80,64},{96,112},{112,96},{1... | collective-permute-start | bytes 884744 | tf_op jit(solution)/shard_map/ppermute | solution.py:46
  18.7 1.5 collective-permute-done
  20.2 0.9 pad_maximum_fusion.1.refs_0_.refs_9_.refs_18_
  21.1 12.8 %all-to-all-done = bf16[16,16,8,128]{3,2,1,0:T(8,128)(2,1)S(1)} async-done(((bf16[16,16,8,128]{3,2,1,0:T(8,128)(2,1)}), bf16[16,16,8,128]{3,2,1,0:T(8,128)(2,1)S(1)}, u32[]{:S(2)}, u32[]{:S(2)}) %all-to-all-start) | async-done | bytes 524320 | tf_op jit(solution)/shard_map/all_to_all | solution.py:220
  33.9 0.0 all-gather.3.cloned.1.call-update
  33.9 0.1 pad_maximum_fusion
  34.0 1.3 copy.15
  35.2 9.5 %all-to-all-start.1 = ((bf16[32,16,8,128]{3,2,1,0:T(8,128)(2,1)}), bf16[32,16,8,128]{3,2,1,0:T(8,128)(2,1)}, u32[]{:S(2)}, u32[]{:S(2)}) async-start(bf16[32,16,8,128]{3,2,1,0:T(8,128)(2,1)} %copy.15), calls=%async_computation.1 | async-start | bytes 2097152 | tf_op jit(solution)/shard_map/all_to_all | solution.py:227
  44.7 0.0 copy-done
  44.8 1.3 collective-permute-start.1
  46.1 36.3 %collective-permute-done.1.refs_8_.refs_17_.refs_26_ = bf16[272,1024]{1,0:T(8,128)(2,1)S(1)} collective-permute-done((bf16[272,1024]{1,0:T(8,128)(2,1)S(1)}, bf16[272,1024]{1,0:T(8,128)(2,1)S(1)}, u32[]{:S(2)}, u32[]{:S(2)}) %collective-permute-start.1) | collective-permute-done | bytes 557088 | tf_op jit(solution)/shard_map/ppermute | solution.py:46
  82.3 1.3 collective-permute-start.2
  83.6 1.3 collective-permute-start.4
  84.9 19.9 %collective-permute-done.2.refs_7_.refs_16_.refs_25_ = bf16[272,1024]{1,0:T(8,128)(2,1)S(1)} collective-permute-done((bf16[272,1024]{1,0:T(8,128)(2,1)S(1)}, bf16[272,1024]{1,0:T(8,128)(2,1)S(1)}, u32[]{:S(2)}, u32[]{:S(2)}) %collective-permute-start.2) | collective-permute-done | bytes 557088 | tf_op jit(solution)/shard_map/ppermute | solution.py:46
  104.8 1.3 collective-permute-start.3
  106.1 0.0 copy-done.10
  106.1 0.0 copy-done.11
  106.1 0.1 select_reduce_fusion
  106.2 0.6 and_select_fusion
  106.8 0.7 and_select_fusion.1.rows_ref
  107.4 10.3 %collective-permute-done.4.refs_5_.refs_14_.refs_23_ = bf16[272,1024]{1,0:T(8,128)(2,1)S(1)} collective-permute-done((bf16[272,1024]{1,0:T(8,128)(2,1)S(1)}, bf16[272,1024]{1,0:T(8,128)(2,1)S(1)}, u32[]{:S(2)}, u32[]{:S(2)}) %collective-permute-start.4) | collective-permute-done | bytes 557088 | tf_op jit(solution)/shard_map/ppermute | solution.py:46
  117.7 0.0 copy-done.3
  117.8 1.3 collective-permute-done.3.refs_6_.refs_15_.refs_24_
  119.1 0.0 copy-done.4
  119.1 0.0 all-to-all-done.1
  119.1 2.5 %pick_images.1 = bf16[32,16,8,128]{3,2,1,0:T(8,128)(2,1)} custom-call(s32[32]{0:T(128)} %and_select_fusion.1.rows_ref, s32[32]{0:T(128)} %get-tuple-element.15.places_ref, bf16[2,16,16,8,128]{4,3,2,1,0:T(8,128)(2,1)} %bitcast.7.table_ref), custom_call_target="tpu_custom_call" | custom-call | bytes 2097152 | tf_op jit(solution)/shard_map/pick_images/pallas_call | solution.py:135
  121.6 0.0 copy-done.2
  121.6 6.7 %all-to-all-start.2 = ((bf16[16,2,16,8,128]{4,3,2,1,0:T(8,128)(2,1)}), bf16[16,2,16,8,128]{4,3,2,1,0:T(8,128)(2,1)S(1)}, u32[]{:S(2)}, u32[]{:S(2)}) async-start(bf16[16,2,16,8,128]{4,3,2,1,0:T(8,128)(2,1)} %bitcast.38), calls=%async_computation.2 | async-start | bytes 2097152 | tf_op jit(solution)/shard_map/all_to_all | solution.py:240
  128.2 0.0 copy-done.5
  128.2 1.1 broadcast_select_fusion
  129.3 2.1 %collective-permute-start.5 = (bf16[128,2048]{1,0:T(8,128)(2,1)}, bf16[128,2048]{1,0:T(8,128)(2,1)S(1)}, u32[]{:S(2)}, u32[]{:S(2)}) collective-permute-start(bf16[128,2048]{1,0:T(8,128)(2,1)} %get-tuple-element.17), channel_id=1, source_target_pairs={{0,16},{16,0},{32,48},{48,32},{64,80},{80,64},{96,112},{112,96},{1... | collective-permute-start | bytes 1572872 | tf_op jit(solution)/shard_map/ppermute | solution.py:46
  131.4 0.6 pad_add_fusion.place_ref
  132.1 1.3 collective-permute-done.5.q_far_ref
  133.3 0.8 copy-done.6
  134.1 14.1 %self_attention.1 = (bf16[128,2048]{1,0:T(8,128)(2,1)}, bf16[128,2048]{1,0:T(8,128)(2,1)}) custom-call(s32[3]{0:T(128)} %pad_add_fusion.place_ref, bf16[128,2048]{1,0:T(8,128)(2,1)} %get-tuple-element.18.q_own_ref, bf16[128,2048]{1,0:T(8,128)(2,1)} %copy-done.6, bf16[272,1024]{1,0:T(8,128)(2,1)} %pad_maximum_fusion.1.refs_0_.refs_9_.refs_18_, ...), custom_call_target="tpu_custom_call" | custom-call | flops 2684354560 | bytes 8388608 | tf_op jit(solution)/shard_map/self_attention/pallas_call | solution.py:106
  148.2 2.1 %collective-permute-start.6 = (bf16[128,2048]{1,0:T(8,128)(2,1)}, bf16[128,2048]{1,0:T(8,128)(2,1)S(1)}, u32[]{:S(2)}, u32[]{:S(2)}) collective-permute-start(bf16[128,2048]{1,0:T(8,128)(2,1)} %get-tuple-element.14), channel_id=1, source_target_pairs={{0,16},{16,0},{32,48},{48,32},{64,80},{80,64},{96,112},{112,96},{1... | collective-permute-start | bytes 1572872 | tf_op jit(solution)/shard_map/ppermute | solution.py:46
  151.1 5.1 %all-to-all-done.2 = bf16[16,2,16,8,128]{4,3,2,1,0:T(8,128)(2,1)S(1)} async-done(((bf16[16,2,16,8,128]{4,3,2,1,0:T(8,128)(2,1)}), bf16[16,2,16,8,128]{4,3,2,1,0:T(8,128)(2,1)S(1)}, u32[]{:S(2)}, u32[]{:S(2)}) %all-to-all-start.2) | async-done | bytes 1048608 | tf_op jit(solution)/shard_map/all_to_all | solution.py:240
  156.2 0.0 collective-permute-done.6.far_ref
  156.2 1.0 copy-done.1
  157.2 0.2 copy-done.8
  157.4 8.4 %cross_attention.1 = bf16[128,4096]{1,0:T(8,128)(2,1)} custom-call(s32[1]{0:T(128)} %bitcast.core_ref, f32[1]{0:T(128)S(6)} %tanh.3.gate_ref, bf16[128,4096]{1,0:T(8,128)(2,1)} %bitcast.42, bf16[16,2,128,128]{3,2,1,0:T(8,128)(2,1)} %bitcast.36, bf16[16,2,128,128]{3,2,1,0:T(8,128)(2,1)} %bitcast.37, bf16[128,2048]{1,0:T(8,128)(2,1)} %get-tuple-element.13.own_ref, ...), custom_call_target="tpu_custom_call" | custom-call | flops 268435456 | bytes 6291456 | tf_op jit(solution)/shard_map/cross_attention/pallas_call | solution.py:174
  (17 shorter events, 0.1 us)
Async XLA Ops:
  7.7 8.9 %copy-start.7 = (bf16[1,128,2048]{2,1,0:T(8,128)(2,1)S(1)}, bf16[1,128,2048]{2,1,0:T(8,128)(2,1)}, u32[]{:S(2)}) copy-start(bf16[1,128,2048]{2,1,0:T(8,128)(2,1)} %param.9) | copy-start | bytes 1572868
  8.6 8.0 %copy-start.9 = (s32[1,128]{1,0:T(1,128)S(1)}, s32[1,128]{1,0:T(1,128)}, u32[]{:S(2)}) copy-start(s32[1,128]{1,0:T(1,128)} %param.10) | copy-start | bytes 1540
  8.6 25.2 %all-to-all-start = ((bf16[16,16,8,128]{3,2,1,0:T(8,128)(2,1)}), bf16[16,16,8,128]{3,2,1,0:T(8,128)(2,1)S(1)}, u32[]{:S(2)}, u32[]{:S(2)}) async-start(bf16[16,16,8,128]{3,2,1,0:T(8,128)(2,1)} %copy.14), calls=%async_computation | async-start | bytes 1048576 | tf_op jit(solution)/shard_map/all_to_all | solution.py:220
  16.6 116.8 %all-gather.3.cloned.1.call-start = ((), (), s32[]{:S(2)}) async-start(), calls=%async_computation.3 | async-start | bytes 5013504 | tf_op jit(solution)/shard_map/all_gather | solution.py:225
  16.7 3.5 %collective-permute-start = (bf16[144,1024]{1,0:T(8,128)(2,1)S(1)}, bf16[144,1024]{1,0:T(8,128)(2,1)S(1)}, u32[]{:S(2)}, u32[]{:S(2)}) collective-permute-start(bf16[144,1024]{1,0:T(8,128)(2,1)S(1)} %fusion.1), channel_id=1, source_target_pairs={{0,16},{16,0},{32,48},{48,32},{64,80},{80,64},{96,112},{112,96},{1... | collective-permute-start | bytes 884744 | tf_op jit(solution)/shard_map/ppermute | solution.py:46
  35.2 9.5 %copy-start = (bf16[272,1024]{1,0:T(8,128)(2,1)S(1)}, bf16[272,1024]{1,0:T(8,128)(2,1)}, u32[]{:S(2)}) copy-start(bf16[272,1024]{1,0:T(8,128)(2,1)} %pad_maximum_fusion.1.refs_0_.refs_9_.refs_18_) | copy-start | bytes 1671172
  35.2 70.8 %copy-start.10 = (s32[1,32]{1,0:T(1,128)S(1)}, s32[1,32]{1,0:T(1,128)}, u32[]{:S(2)}) copy-start(s32[1,32]{1,0:T(1,128)} %param.14) | copy-start | bytes 388
  35.2 70.9 %copy-start.11 = (s32[1,64]{1,0:T(1,128)S(1)}, s32[1,64]{1,0:T(1,128)}, u32[]{:S(2)}) copy-start(s32[1,64]{1,0:T(1,128)} %param.13) | copy-start | bytes 772
  35.2 83.8 %all-to-all-start.1 = ((bf16[32,16,8,128]{3,2,1,0:T(8,128)(2,1)}), bf16[32,16,8,128]{3,2,1,0:T(8,128)(2,1)}, u32[]{:S(2)}, u32[]{:S(2)}) async-start(bf16[32,16,8,128]{3,2,1,0:T(8,128)(2,1)} %copy.15), calls=%async_computation.1 | async-start | bytes 2097152 | tf_op jit(solution)/shard_map/all_to_all | solution.py:227
  44.8 37.6 %collective-permute-start.1 = (bf16[272,1024]{1,0:T(8,128)(2,1)S(1)}, bf16[272,1024]{1,0:T(8,128)(2,1)S(1)}, u32[]{:S(2)}, u32[]{:S(2)}) collective-permute-start(bf16[272,1024]{1,0:T(8,128)(2,1)S(1)} %copy-done), channel_id=1, source_target_pairs={{128,256},{144,272},{160,288},{176,304},{192,320},{208,336},{224,3... | collective-permute-start | bytes 1671176 | tf_op jit(solution)/shard_map/ppermute | solution.py:46
  82.3 39.2 %copy-start.2 = (bf16[272,1024]{1,0:T(8,128)(2,1)}, bf16[272,1024]{1,0:T(8,128)(2,1)S(1)}, u32[]{:S(2)}) copy-start(bf16[272,1024]{1,0:T(8,128)(2,1)S(1)} %collective-permute-done.1.refs_8_.refs_17_.refs_26_) | copy-start | bytes 1671172
  82.3 22.4 %collective-permute-start.2 = (bf16[272,1024]{1,0:T(8,128)(2,1)S(1)}, bf16[272,1024]{1,0:T(8,128)(2,1)S(1)}, u32[]{:S(2)}, u32[]{:S(2)}) collective-permute-start(bf16[272,1024]{1,0:T(8,128)(2,1)S(1)} %collective-permute-done.1.refs_8_.refs_17_.refs_26_), channel_id=1, source_target_pairs={{288,256},{304,272},{320,288},{336,304},{352,320},{368,336},{289,2... | collective-permute-start | bytes 1671176 | tf_op jit(solution)/shard_map/ppermute | solution.py:46
  83.6 34.1 %collective-permute-start.4 = (bf16[272,1024]{1,0:T(8,128)(2,1)S(1)}, bf16[272,1024]{1,0:T(8,128)(2,1)S(1)}, u32[]{:S(2)}, u32[]{:S(2)}) collective-permute-start(bf16[272,1024]{1,0:T(8,128)(2,1)S(1)} %copy-done), channel_id=1, source_target_pairs={{224,256},{240,272},{225,257},{241,273},{226,258},{242,274},{227,2... | collective-permute-start | bytes 1671176 | tf_op jit(solution)/shard_map/ppermute | solution.py:46
  104.8 13.0 %copy-start.3 = (bf16[272,1024]{1,0:T(8,128)(2,1)}, bf16[272,1024]{1,0:T(8,128)(2,1)S(1)}, u32[]{:S(2)}) copy-start(bf16[272,1024]{1,0:T(8,128)(2,1)S(1)} %collective-permute-done.2.refs_7_.refs_16_.refs_25_) | copy-start | bytes 1671172
  104.8 14.3 %collective-permute-start.3 = (bf16[272,1024]{1,0:T(8,128)(2,1)S(1)}, bf16[272,1024]{1,0:T(8,128)(2,1)}, u32[]{:S(2)}, u32[]{:S(2)}) collective-permute-start(bf16[272,1024]{1,0:T(8,128)(2,1)S(1)} %collective-permute-done.2.refs_7_.refs_16_.refs_25_), channel_id=1, source_target_pairs={{288,256},{304,272},{320,288},{336,304},{289,257},{305,273},{321,2... | collective-permute-start | bytes 1671176 | tf_op jit(solution)/shard_map/ppermute | solution.py:46
  117.8 1.3 copy-start.4
  121.6 6.7 %copy-start.5 = (bf16[1,128,4096]{2,1,0:T(8,128)(2,1)S(1)}, bf16[1,128,4096]{2,1,0:T(8,128)(2,1)}, u32[]{:S(2)}) copy-start(bf16[1,128,4096]{2,1,0:T(8,128)(2,1)} %param.8) | copy-start | bytes 3145732
  121.6 34.6 %all-to-all-start.2 = ((bf16[16,2,16,8,128]{4,3,2,1,0:T(8,128)(2,1)}), bf16[16,2,16,8,128]{4,3,2,1,0:T(8,128)(2,1)S(1)}, u32[]{:S(2)}, u32[]{:S(2)}) async-start(bf16[16,2,16,8,128]{4,3,2,1,0:T(8,128)(2,1)} %bitcast.38), calls=%async_computation.2 | async-start | bytes 2097152 | tf_op jit(solution)/shard_map/all_to_all | solution.py:240
  129.3 4.0 %collective-permute-start.5 = (bf16[128,2048]{1,0:T(8,128)(2,1)}, bf16[128,2048]{1,0:T(8,128)(2,1)S(1)}, u32[]{:S(2)}, u32[]{:S(2)}) collective-permute-start(bf16[128,2048]{1,0:T(8,128)(2,1)} %get-tuple-element.17), channel_id=1, source_target_pairs={{0,16},{16,0},{32,48},{48,32},{64,80},{80,64},{96,112},{112,96},{1... | collective-permute-start | bytes 1572872 | tf_op jit(solution)/shard_map/ppermute | solution.py:46
  133.3 0.8 copy-start.6
  148.2 8.0 %collective-permute-start.6 = (bf16[128,2048]{1,0:T(8,128)(2,1)}, bf16[128,2048]{1,0:T(8,128)(2,1)S(1)}, u32[]{:S(2)}, u32[]{:S(2)}) collective-permute-start(bf16[128,2048]{1,0:T(8,128)(2,1)} %get-tuple-element.14), channel_id=1, source_target_pairs={{0,16},{16,0},{32,48},{48,32},{64,80},{80,64},{96,112},{112,96},{1... | collective-permute-start | bytes 1572872 | tf_op jit(solution)/shard_map/ppermute | solution.py:46
  156.2 1.0 copy-start.1
  156.2 1.2 copy-start.8
Sparse Core Ops, SparseCore 0:
  34.0 56.5 all-gather.2

commit v2 on v1

--- a/solution.py
+++ b/solution.py
@@ -76,19 +76,17 @@
 
     key = jnp.concatenate(window(keys, lambda block: block), 0)
     value = jnp.concatenate(window(values, lambda block: block), 0)
+    value = jnp.concatenate([value, jnp.ones_like(value)], 1)
     rows = q_own_ref.shape[0]
     for h in range(GROUP):
         cols = slice(h * DIM, (h + 1) * DIM)
-        query = jnp.concatenate([q_own_ref[:, cols], q_far_ref[:, cols]], 0)
-        s = lax.dot_general(query, key, (((1,), (1,)), ((), ())), preferred_element_type=jnp.float32)
-        s = s + bias_ref[...]
-        top = jnp.max(s, axis=1, keepdims=True)
-        w = jnp.exp2((s - top) * EXP2_SCALE)
-        den = jnp.sum(w, axis=1, keepdims=True)
-        num = jnp.dot(w.astype(jnp.bfloat16), value, preferred_element_type=jnp.float32)
-        ctx = (num / den).astype(jnp.bfloat16)
-        out_own_ref[:, cols] = ctx[:rows]
-        out_far_ref[:, cols] = ctx[rows:]
+        for part, (q_ref, out_ref) in enumerate(((q_own_ref, out_own_ref), (q_far_ref, out_far_ref))):
+            s = lax.dot_general(q_ref[:, cols], key, (((1,), (1,)), ((), ())), preferred_element_type=jnp.float32)
+            s = s + bias_ref[part * rows : (part + 1) * rows, :]
+            top = jnp.max(s, axis=1, keepdims=True)
+            w = jnp.exp2((s - top) * EXP2_SCALE).astype(jnp.bfloat16)
+            num = jnp.dot(w, value, preferred_element_type=jnp.float32)
+            out_ref[:, cols] = (num[:, :DIM] / num[:, DIM:]).astype(jnp.bfloat16)
 
 
 def self_attention(place, q_own, q_far, own, line, across):
@@ -144,42 +142,43 @@
 
 
 def cross_kernel(core_ref, gate_ref, q_ref, key_ref, value_ref, own_ref, far_ref, out_ref):
-    here = (pl.program_id(0) // (KV_HEADS // CORES)) == core_ref[0]
+    here = pl.program_id(0) == core_ref[0]
     gate = gate_ref[0]
-    spans = key_ref.shape[1]
+    heads, spans = key_ref.shape[:2]
     span = q_ref.shape[0] // spans
-    for j in range(spans):
-        rows = slice(j * span, (j + 1) * span)
-        q = jnp.concatenate([q_ref[rows, h * DIM : (h + 1) * DIM] for h in range(GROUP)], 0)
-        s = lax.dot_general(q, key_ref[0, j], (((1,), (1,)), ((), ())), preferred_element_type=jnp.float32)
-        top = jnp.max(s, axis=1, keepdims=True)
-        w = jnp.exp2((s - top) * EXP2_SCALE)
-        den = jnp.sum(w, axis=1, keepdims=True)
-        num = jnp.dot(w.astype(jnp.bfloat16), value_ref[0, j], preferred_element_type=jnp.float32)
-        cross = (num / den).astype(jnp.bfloat16).astype(jnp.float32)
-        for h in range(GROUP):
-            cols = slice(h * DIM, (h + 1) * DIM)
-            own, far = own_ref[rows, cols].astype(jnp.float32), far_ref[rows, cols].astype(jnp.float32)
-            mixed = jnp.where(here, own, far) + gate * cross[h * span : (h + 1) * span]
-            out_ref[rows, cols] = mixed.astype(jnp.bfloat16)
+    for g in range(heads):
+        for j in range(spans):
+            rows = slice(j * span, (j + 1) * span)
+            places = [slice((g * GROUP + h) * DIM, (g * GROUP + h + 1) * DIM) for h in range(GROUP)]
+            q = jnp.concatenate([q_ref[rows, cols] for cols in places], 0)
+            s = lax.dot_general(q, key_ref[g, j], (((1,), (1,)), ((), ())), preferred_element_type=jnp.float32)
+            top = jnp.max(s, axis=1, keepdims=True)
+            w = jnp.exp2((s - top) * EXP2_SCALE)
+            den = jnp.sum(w, axis=1, keepdims=True)
+            num = jnp.dot(w.astype(jnp.bfloat16), value_ref[g, j], preferred_element_type=jnp.float32)
+            cross = (num / den).astype(jnp.bfloat16).astype(jnp.float32)
+            for h, cols in enumerate(places):
+                own, far = own_ref[rows, cols].astype(jnp.float32), far_ref[rows, cols].astype(jnp.float32)
+                mixed = jnp.where(here, own, far) + gate * cross[h * span : (h + 1) * span]
+                out_ref[rows, cols] = mixed.astype(jnp.bfloat16)
 
 
 def cross_attention(core, gate, cross_q, images, own, far):
     tokens, width = cross_q.shape
     half = KV_HEADS // CORES
     smem = pl.BlockSpec(memory_space=pltpu.SMEM)
-    q_spec = pl.BlockSpec((tokens, GROUP * DIM), lambda g: (0, g))
-    half_spec = pl.BlockSpec((tokens, GROUP * DIM), lambda g: (0, g % half))
-    image = (1,) + images.shape[1:]
+    q_spec = pl.BlockSpec((tokens, width // CORES), lambda c: (0, c))
+    half_spec = pl.BlockSpec((tokens, width // CORES), lambda c: (0, 0))
+    image = (half,) + images.shape[1:]
     return pl.pallas_call(
         cross_kernel,
-        grid=(KV_HEADS,),
+        grid=(CORES,),
         in_specs=[
             smem,
             smem,
             q_spec,
-            pl.BlockSpec(image, lambda g: (g, 0, 0, 0)),
-            pl.BlockSpec(image, lambda g: (KV_HEADS + g, 0, 0, 0)),
+            pl.BlockSpec(image, lambda c: (c, 0, 0, 0)),
+            pl.BlockSpec(image, lambda c: (CORES + c, 0, 0, 0)),
             half_spec,
             half_spec,
         ],

time: 174 us -> 169 us (0.971)
  Pallas kernels: 25 us -> 19.1 us
  waiting for transfers between devices: 88.4 us -> 90.4 us
    pallas_call x1, Pallas kernels: 8.44 us -> 4.51 us  [cross_attention(): pl.pallas_call(cross_kernel, grid=(CORES,), in_specs=[smem, smem, q_spec,...]
    all_to_all x1, waiting for transfers between devices: 5.15 us -> 7.14 us  [on_device(): images = lax.all_to_all(chosen, ('y', 'core'), 0, 0, tiled=True)]
    pallas_call x1, Pallas kernels: 14.1 us -> 12.1 us  [self_attention(): pl.pallas_call(self_kernel, grid_spec=pltpu.PrefetchScalarGridSpec(num_sc...]
  transfers between devices with their start and end apart: 11 -> 11, of which waited for: 8 -> 8; matrix products, arithmetic and copies ran while one was open for 3% -> 3% of each run, Pallas kernels for 10% -> 9%
where the time goes in v2:
time: 169 us
  waiting for transfers between devices  90.4 us (53%)
  starting transfers between devices  35.5 us (21%)
  Pallas kernels  19.1 us (11%)
  between operations  14.3 us (8%)
  local copies, waits for them, and re-layouts  5.37 us (3%)
  other arithmetic  4.02 us (2%)
    ppermute x7, waiting for transfers between devices, move(): return lax.ppermute(value, SEQ, perm)  70.5 us
    all_to_all x1, waiting for transfers between devices, on_device(): spread = lax.all_to_all(image, ('y', 'core'), 0, 0, tiled=True)  12.8 us
    pallas_call x1, Pallas kernels, self_attention(): pl.pallas_call(self_kernel, grid_spec=pltpu.PrefetchScalarGridSpec(num_sc...  12.1 us
    ppermute x7, starting transfers between devices, move(): return lax.ppermute(value, SEQ, perm)  11.4 us
    all_to_all x1, starting transfers between devices, on_device(): lax.all_to_all(jnp.concatenate([spread, spread], 0), ('zh',) + DOC, 0, 0,...  9.49 us
    all_to_all x1, starting transfers between devices, on_device(): spread = lax.all_to_all(image, ('y', 'core'), 0, 0, tiled=True)  7.92 us
    all_to_all x1, waiting for transfers between devices, on_device(): images = lax.all_to_all(chosen, ('y', 'core'), 0, 0, tiled=True)  7.14 us
    all_to_all x1, starting transfers between devices, on_device(): images = lax.all_to_all(chosen, ('y', 'core'), 0, 0, tiled=True)  6.66 us
  transfers between devices with their start and end apart: 11, of which 8 were waited for; matrix products, arithmetic and copies ran while one was open for 3% of the time, Pallas kernels for 9%

profile of v2, /device:TPU:257, one launch (start us, length us, event | category | flops | bytes accessed | tf_op | source)
XLA Modules:
  0.0 168.8 jit_solution(12660892791931447846)
XLA Ops:
  6.5 1.1 copy.18
  7.7 0.0 copy-start.7
  7.7 0.9 copy.14
  8.6 7.9 %all-to-all-start = ((bf16[16,16,8,128]{3,2,1,0:T(8,128)(2,1)}), bf16[16,16,8,128]{3,2,1,0:T(8,128)(2,1)S(1)}, u32[]{:S(2)}, u32[]{:S(2)}) async-start(bf16[16,16,8,128]{3,2,1,0:T(8,128)(2,1)} %copy.14), calls=%async_computation | async-start | bytes 1048576 | tf_op jit(solution)/shard_map/all_to_all | solution.py:219
  16.6 0.0 all-gather.3.cloned.1.call-start
  16.6 0.0 copy-done.7
  16.7 0.0 copy-done.9
  16.7 2.0 %collective-permute-start = (bf16[144,1024]{1,0:T(8,128)(2,1)S(1)}, bf16[144,1024]{1,0:T(8,128)(2,1)S(1)}, u32[]{:S(2)}, u32[]{:S(2)}) collective-permute-start(bf16[144,1024]{1,0:T(8,128)(2,1)S(1)} %fusion.1), channel_id=1, source_target_pairs={{0,16},{16,0},{32,48},{48,32},{64,80},{80,64},{96,112},{112,96},{1... | collective-permute-start | bytes 884744 | tf_op jit(solution)/shard_map/ppermute | solution.py:46
  18.7 1.5 collective-permute-done
  20.2 0.9 pad_maximum_fusion.1.refs_0_.refs_9_.refs_18_
  21.1 12.8 %all-to-all-done = bf16[16,16,8,128]{3,2,1,0:T(8,128)(2,1)S(1)} async-done(((bf16[16,16,8,128]{3,2,1,0:T(8,128)(2,1)}), bf16[16,16,8,128]{3,2,1,0:T(8,128)(2,1)S(1)}, u32[]{:S(2)}, u32[]{:S(2)}) %all-to-all-start) | async-done | bytes 524320 | tf_op jit(solution)/shard_map/all_to_all | solution.py:219
  33.9 0.0 all-gather.3.cloned.1.call-update
  33.9 0.1 pad_maximum_fusion
  34.0 1.3 copy.15
  35.2 9.5 %all-to-all-start.1 = ((bf16[32,16,8,128]{3,2,1,0:T(8,128)(2,1)}), bf16[32,16,8,128]{3,2,1,0:T(8,128)(2,1)}, u32[]{:S(2)}, u32[]{:S(2)}) async-start(bf16[32,16,8,128]{3,2,1,0:T(8,128)(2,1)} %copy.15), calls=%async_computation.1 | async-start | bytes 2097152 | tf_op jit(solution)/shard_map/all_to_all | solution.py:226
  44.7 0.0 copy-done
  44.8 1.3 collective-permute-start.1
  46.1 36.3 %collective-permute-done.1.refs_8_.refs_17_.refs_26_ = bf16[272,1024]{1,0:T(8,128)(2,1)S(1)} collective-permute-done((bf16[272,1024]{1,0:T(8,128)(2,1)S(1)}, bf16[272,1024]{1,0:T(8,128)(2,1)S(1)}, u32[]{:S(2)}, u32[]{:S(2)}) %collective-permute-start.1) | collective-permute-done | bytes 557088 | tf_op jit(solution)/shard_map/ppermute | solution.py:46
  82.3 1.3 collective-permute-start.2
  83.6 1.3 collective-permute-start.4
  84.9 19.9 %collective-permute-done.2.refs_7_.refs_16_.refs_25_ = bf16[272,1024]{1,0:T(8,128)(2,1)S(1)} collective-permute-done((bf16[272,1024]{1,0:T(8,128)(2,1)S(1)}, bf16[272,1024]{1,0:T(8,128)(2,1)S(1)}, u32[]{:S(2)}, u32[]{:S(2)}) %collective-permute-start.2) | collective-permute-done | bytes 557088 | tf_op jit(solution)/shard_map/ppermute | solution.py:46
  104.8 1.3 collective-permute-start.3
  106.1 0.0 copy-done.10
  106.1 0.0 copy-done.11
  106.1 0.1 select_reduce_fusion
  106.2 0.6 and_select_fusion
  106.8 0.7 and_select_fusion.1.rows_ref
  107.4 10.3 %collective-permute-done.4.refs_5_.refs_14_.refs_23_ = bf16[272,1024]{1,0:T(8,128)(2,1)S(1)} collective-permute-done((bf16[272,1024]{1,0:T(8,128)(2,1)S(1)}, bf16[272,1024]{1,0:T(8,128)(2,1)S(1)}, u32[]{:S(2)}, u32[]{:S(2)}) %collective-permute-start.4) | collective-permute-done | bytes 557088 | tf_op jit(solution)/shard_map/ppermute | solution.py:46
  117.7 0.0 copy-done.3
  117.8 1.3 collective-permute-done.3.refs_6_.refs_15_.refs_24_
  119.1 0.0 copy-done.4
  119.1 0.0 all-to-all-done.1
  119.1 2.5 %pick_images.1 = bf16[32,16,8,128]{3,2,1,0:T(8,128)(2,1)} custom-call(s32[32]{0:T(128)} %and_select_fusion.1.rows_ref, s32[32]{0:T(128)} %get-tuple-element.15.places_ref, bf16[2,16,16,8,128]{4,3,2,1,0:T(8,128)(2,1)} %bitcast.7.table_ref), custom_call_target="tpu_custom_call" | custom-call | bytes 2097152 | tf_op jit(solution)/shard_map/pick_images/pallas_call | solution.py:133
  121.6 0.0 copy-done.2
  121.6 6.7 %all-to-all-start.2 = ((bf16[16,2,16,8,128]{4,3,2,1,0:T(8,128)(2,1)}), bf16[16,2,16,8,128]{4,3,2,1,0:T(8,128)(2,1)S(1)}, u32[]{:S(2)}, u32[]{:S(2)}) async-start(bf16[16,2,16,8,128]{4,3,2,1,0:T(8,128)(2,1)} %bitcast.38), calls=%async_computation.2 | async-start | bytes 2097152 | tf_op jit(solution)/shard_map/all_to_all | solution.py:239
  128.2 0.0 copy-done.5
  128.2 1.1 broadcast_select_fusion
  129.3 2.1 %collective-permute-start.5 = (bf16[128,2048]{1,0:T(8,128)(2,1)}, bf16[128,2048]{1,0:T(8,128)(2,1)S(1)}, u32[]{:S(2)}, u32[]{:S(2)}) collective-permute-start(bf16[128,2048]{1,0:T(8,128)(2,1)} %get-tuple-element.17), channel_id=1, source_target_pairs={{0,16},{16,0},{32,48},{48,32},{64,80},{80,64},{96,112},{112,96},{1... | collective-permute-start | bytes 1572872 | tf_op jit(solution)/shard_map/ppermute | solution.py:46
  131.5 0.6 pad_add_fusion.place_ref
  132.1 1.3 collective-permute-done.5.q_far_ref
  133.3 0.8 copy-done.6
  134.1 12.1 %self_attention.1 = (bf16[128,2048]{1,0:T(8,128)(2,1)}, bf16[128,2048]{1,0:T(8,128)(2,1)}) custom-call(s32[3]{0:T(128)} %pad_add_fusion.place_ref, bf16[128,2048]{1,0:T(8,128)(2,1)} %get-tuple-element.18.q_own_ref, bf16[128,2048]{1,0:T(8,128)(2,1)} %copy-done.6, bf16[272,1024]{1,0:T(8,128)(2,1)} %pad_maximum_fusion.1.refs_0_.refs_9_.refs_18_, ...), custom_call_target="tpu_custom_call" | custom-call | flops 2684354560 | bytes 8388608 | tf_op jit(solution)/shard_map/self_attention/pallas_call | solution.py:104
  146.3 2.1 %collective-permute-start.6 = (bf16[128,2048]{1,0:T(8,128)(2,1)}, bf16[128,2048]{1,0:T(8,128)(2,1)S(1)}, u32[]{:S(2)}, u32[]{:S(2)}) collective-permute-start(bf16[128,2048]{1,0:T(8,128)(2,1)} %get-tuple-element.14), channel_id=1, source_target_pairs={{0,16},{16,0},{32,48},{48,32},{64,80},{80,64},{96,112},{112,96},{1... | collective-permute-start | bytes 1572872 | tf_op jit(solution)/shard_map/ppermute | solution.py:46
  149.1 7.1 %all-to-all-done.2 = bf16[16,2,16,8,128]{4,3,2,1,0:T(8,128)(2,1)S(1)} async-done(((bf16[16,2,16,8,128]{4,3,2,1,0:T(8,128)(2,1)}), bf16[16,2,16,8,128]{4,3,2,1,0:T(8,128)(2,1)S(1)}, u32[]{:S(2)}, u32[]{:S(2)}) %all-to-all-start.2) | async-done | bytes 1048608 | tf_op jit(solution)/shard_map/all_to_all | solution.py:239
  156.2 0.0 collective-permute-done.6.far_ref
  156.2 1.0 copy-done.1
  157.2 0.2 copy-done.8
  157.4 4.5 %cross_attention.1 = bf16[128,4096]{1,0:T(8,128)(2,1)} custom-call(s32[1]{0:T(128)} %bitcast.core_ref, f32[1]{0:T(128)S(6)} %tanh.3.gate_ref, bf16[128,4096]{1,0:T(8,128)(2,1)} %bitcast.42, bf16[16,2,128,128]{3,2,1,0:T(8,128)(2,1)} %bitcast.36, bf16[16,2,128,128]{3,2,1,0:T(8,128)(2,1)} %bitcast.37, bf16[128,2048]{1,0:T(8,128)(2,1)} %get-tuple-element.13.own_ref, ...), custom_call_target="tpu_custom_call" | custom-call | flops 268435456 | bytes 6291456 | tf_op jit(solution)/shard_map/cross_attention/pallas_call | solution.py:173
  (17 shorter events, 0.1 us)
Async XLA Ops:
  7.7 8.9 %copy-start.7 = (bf16[1,128,2048]{2,1,0:T(8,128)(2,1)S(1)}, bf16[1,128,2048]{2,1,0:T(8,128)(2,1)}, u32[]{:S(2)}) copy-start(bf16[1,128,2048]{2,1,0:T(8,128)(2,1)} %param.9) | copy-start | bytes 1572868
  8.6 8.0 %copy-start.9 = (s32[1,128]{1,0:T(1,128)S(1)}, s32[1,128]{1,0:T(1,128)}, u32[]{:S(2)}) copy-start(s32[1,128]{1,0:T(1,128)} %param.10) | copy-start | bytes 1540
  8.6 25.2 %all-to-all-start = ((bf16[16,16,8,128]{3,2,1,0:T(8,128)(2,1)}), bf16[16,16,8,128]{3,2,1,0:T(8,128)(2,1)S(1)}, u32[]{:S(2)}, u32[]{:S(2)}) async-start(bf16[16,16,8,128]{3,2,1,0:T(8,128)(2,1)} %copy.14), calls=%async_computation | async-start | bytes 1048576 | tf_op jit(solution)/shard_map/all_to_all | solution.py:219
  16.6 116.8 %all-gather.3.cloned.1.call-start = ((), (), s32[]{:S(2)}) async-start(), calls=%async_computation.3 | async-start | bytes 5013504 | tf_op jit(solution)/shard_map/all_gather | solution.py:224
  16.7 3.5 %collective-permute-start = (bf16[144,1024]{1,0:T(8,128)(2,1)S(1)}, bf16[144,1024]{1,0:T(8,128)(2,1)S(1)}, u32[]{:S(2)}, u32[]{:S(2)}) collective-permute-start(bf16[144,1024]{1,0:T(8,128)(2,1)S(1)} %fusion.1), channel_id=1, source_target_pairs={{0,16},{16,0},{32,48},{48,32},{64,80},{80,64},{96,112},{112,96},{1... | collective-permute-start | bytes 884744 | tf_op jit(solution)/shard_map/ppermute | solution.py:46
  35.2 9.5 %copy-start = (bf16[272,1024]{1,0:T(8,128)(2,1)S(1)}, bf16[272,1024]{1,0:T(8,128)(2,1)}, u32[]{:S(2)}) copy-start(bf16[272,1024]{1,0:T(8,128)(2,1)} %pad_maximum_fusion.1.refs_0_.refs_9_.refs_18_) | copy-start | bytes 1671172
  35.2 70.8 %copy-start.10 = (s32[1,32]{1,0:T(1,128)S(1)}, s32[1,32]{1,0:T(1,128)}, u32[]{:S(2)}) copy-start(s32[1,32]{1,0:T(1,128)} %param.14) | copy-start | bytes 388
  35.2 70.9 %copy-start.11 = (s32[1,64]{1,0:T(1,128)S(1)}, s32[1,64]{1,0:T(1,128)}, u32[]{:S(2)}) copy-start(s32[1,64]{1,0:T(1,128)} %param.13) | copy-start | bytes 772
  35.2 83.8 %all-to-all-start.1 = ((bf16[32,16,8,128]{3,2,1,0:T(8,128)(2,1)}), bf16[32,16,8,128]{3,2,1,0:T(8,128)(2,1)}, u32[]{:S(2)}, u32[]{:S(2)}) async-start(bf16[32,16,8,128]{3,2,1,0:T(8,128)(2,1)} %copy.15), calls=%async_computation.1 | async-start | bytes 2097152 | tf_op jit(solution)/shard_map/all_to_all | solution.py:226
  44.8 37.6 %collective-permute-start.1 = (bf16[272,1024]{1,0:T(8,128)(2,1)S(1)}, bf16[272,1024]{1,0:T(8,128)(2,1)S(1)}, u32[]{:S(2)}, u32[]{:S(2)}) collective-permute-start(bf16[272,1024]{1,0:T(8,128)(2,1)S(1)} %copy-done), channel_id=1, source_target_pairs={{128,256},{144,272},{160,288},{176,304},{192,320},{208,336},{224,3... | collective-permute-start | bytes 1671176 | tf_op jit(solution)/shard_map/ppermute | solution.py:46
  82.3 39.2 %copy-start.2 = (bf16[272,1024]{1,0:T(8,128)(2,1)}, bf16[272,1024]{1,0:T(8,128)(2,1)S(1)}, u32[]{:S(2)}) copy-start(bf16[272,1024]{1,0:T(8,128)(2,1)S(1)} %collective-permute-done.1.refs_8_.refs_17_.refs_26_) | copy-start | bytes 1671172
  82.3 22.4 %collective-permute-start.2 = (bf16[272,1024]{1,0:T(8,128)(2,1)S(1)}, bf16[272,1024]{1,0:T(8,128)(2,1)S(1)}, u32[]{:S(2)}, u32[]{:S(2)}) collective-permute-start(bf16[272,1024]{1,0:T(8,128)(2,1)S(1)} %collective-permute-done.1.refs_8_.refs_17_.refs_26_), channel_id=1, source_target_pairs={{288,256},{304,272},{320,288},{336,304},{352,320},{368,336},{289,2... | collective-permute-start | bytes 1671176 | tf_op jit(solution)/shard_map/ppermute | solution.py:46
  83.6 34.1 %collective-permute-start.4 = (bf16[272,1024]{1,0:T(8,128)(2,1)S(1)}, bf16[272,1024]{1,0:T(8,128)(2,1)S(1)}, u32[]{:S(2)}, u32[]{:S(2)}) collective-permute-start(bf16[272,1024]{1,0:T(8,128)(2,1)S(1)} %copy-done), channel_id=1, source_target_pairs={{224,256},{240,272},{225,257},{241,273},{226,258},{242,274},{227,2... | collective-permute-start | bytes 1671176 | tf_op jit(solution)/shard_map/ppermute | solution.py:46
  104.8 13.0 %copy-start.3 = (bf16[272,1024]{1,0:T(8,128)(2,1)}, bf16[272,1024]{1,0:T(8,128)(2,1)S(1)}, u32[]{:S(2)}) copy-start(bf16[272,1024]{1,0:T(8,128)(2,1)S(1)} %collective-permute-done.2.refs_7_.refs_16_.refs_25_) | copy-start | bytes 1671172
  104.8 14.3 %collective-permute-start.3 = (bf16[272,1024]{1,0:T(8,128)(2,1)S(1)}, bf16[272,1024]{1,0:T(8,128)(2,1)}, u32[]{:S(2)}, u32[]{:S(2)}) collective-permute-start(bf16[272,1024]{1,0:T(8,128)(2,1)S(1)} %collective-permute-done.2.refs_7_.refs_16_.refs_25_), channel_id=1, source_target_pairs={{288,256},{304,272},{320,288},{336,304},{289,257},{305,273},{321,2... | collective-permute-start | bytes 1671176 | tf_op jit(solution)/shard_map/ppermute | solution.py:46
  117.8 1.3 copy-start.4
  121.6 6.7 %copy-start.5 = (bf16[1,128,4096]{2,1,0:T(8,128)(2,1)S(1)}, bf16[1,128,4096]{2,1,0:T(8,128)(2,1)}, u32[]{:S(2)}) copy-start(bf16[1,128,4096]{2,1,0:T(8,128)(2,1)} %param.8) | copy-start | bytes 3145732
  121.6 34.6 %all-to-all-start.2 = ((bf16[16,2,16,8,128]{4,3,2,1,0:T(8,128)(2,1)}), bf16[16,2,16,8,128]{4,3,2,1,0:T(8,128)(2,1)S(1)}, u32[]{:S(2)}, u32[]{:S(2)}) async-start(bf16[16,2,16,8,128]{4,3,2,1,0:T(8,128)(2,1)} %bitcast.38), calls=%async_computation.2 | async-start | bytes 2097152 | tf_op jit(solution)/shard_map/all_to_all | solution.py:239
  129.3 4.0 %collective-permute-start.5 = (bf16[128,2048]{1,0:T(8,128)(2,1)}, bf16[128,2048]{1,0:T(8,128)(2,1)S(1)}, u32[]{:S(2)}, u32[]{:S(2)}) collective-permute-start(bf16[128,2048]{1,0:T(8,128)(2,1)} %get-tuple-element.17), channel_id=1, source_target_pairs={{0,16},{16,0},{32,48},{48,32},{64,80},{80,64},{96,112},{112,96},{1... | collective-permute-start | bytes 1572872 | tf_op jit(solution)/shard_map/ppermute | solution.py:46
  133.3 0.8 copy-start.6
  146.3 10.0 %collective-permute-start.6 = (bf16[128,2048]{1,0:T(8,128)(2,1)}, bf16[128,2048]{1,0:T(8,128)(2,1)S(1)}, u32[]{:S(2)}, u32[]{:S(2)}) collective-permute-start(bf16[128,2048]{1,0:T(8,128)(2,1)} %get-tuple-element.14), channel_id=1, source_target_pairs={{0,16},{16,0},{32,48},{48,32},{64,80},{80,64},{96,112},{112,96},{1... | collective-permute-start | bytes 1572872 | tf_op jit(solution)/shard_map/ppermute | solution.py:46
  156.2 1.0 copy-start.1
  156.2 1.2 copy-start.8
Sparse Core Ops, SparseCore 0:
  34.0 56.5 all-gather.2

commit v3 on v2

--- a/solution.py
+++ b/solution.py
@@ -1,3 +1,4 @@
+import functools
 import math
 
 import jax
@@ -46,10 +47,12 @@
     return lax.ppermute(value, SEQ, perm)
 
 
-def self_kernel(place_ref, q_own_ref, q_far_ref, *refs):
+def self_kernel(part, place_ref, q_ref, *refs):
     count = 2 * HOPS + 1
     keys, values, ids = refs[:count], refs[count : 2 * count], refs[2 * count : 3 * count]
-    out_own_ref, out_far_ref, bias_ref = refs[3 * count :]
+    out_ref, bias_ref = refs[3 * count :]
+    tokens = q_ref.shape[0]
+    rows = slice(part * tokens, (part + 1) * tokens)
     span = keys[0].shape[0]
     row, y, core = place_ref[0], place_ref[1], place_ref[2]
 
@@ -62,10 +65,11 @@
     @pl.when(pl.program_id(0) == 0)
     def _():
         numbers = window(ids, lambda block: jnp.broadcast_to(block[0:1].astype(jnp.float32), (span, span)))
-        of_query = numbers[0].T
+        of_query = numbers[0].T[rows]
+        numbers = [number[:tokens] for number in numbers]
         own_half = core * (span // CORES)
-        q_at = lax.broadcasted_iota(jnp.int32, (span, span), 0) ^ own_half
-        k_at = lax.broadcasted_iota(jnp.int32, (span, span), 1) ^ own_half
+        q_at = (lax.broadcasted_iota(jnp.int32, (tokens, span), 0) + part * tokens) ^ own_half
+        k_at = lax.broadcasted_iota(jnp.int32, (tokens, span), 1) ^ own_half
         for hop in range(HOPS + 1):
             seen = numbers[hop] == of_query
             if hop == 0:
@@ -77,20 +81,18 @@
     key = jnp.concatenate(window(keys, lambda block: block), 0)
     value = jnp.concatenate(window(values, lambda block: block), 0)
     value = jnp.concatenate([value, jnp.ones_like(value)], 1)
-    rows = q_own_ref.shape[0]
     for h in range(GROUP):
         cols = slice(h * DIM, (h + 1) * DIM)
-        for part, (q_ref, out_ref) in enumerate(((q_own_ref, out_own_ref), (q_far_ref, out_far_ref))):
-            s = lax.dot_general(q_ref[:, cols], key, (((1,), (1,)), ((), ())), preferred_element_type=jnp.float32)
-            s = s + bias_ref[part * rows : (part + 1) * rows, :]
-            top = jnp.max(s, axis=1, keepdims=True)
-            w = jnp.exp2((s - top) * EXP2_SCALE).astype(jnp.bfloat16)
-            num = jnp.dot(w, value, preferred_element_type=jnp.float32)
-            out_ref[:, cols] = (num[:, :DIM] / num[:, DIM:]).astype(jnp.bfloat16)
-
-
-def self_attention(place, q_own, q_far, own, line, across):
-    tokens, width = q_own.shape
+        s = lax.dot_general(q_ref[:, cols], key, (((1,), (1,)), ((), ())), preferred_element_type=jnp.float32)
+        s = s + bias_ref[...]
+        top = jnp.max(s, axis=1, keepdims=True)
+        w = jnp.exp2((s - top) * EXP2_SCALE).astype(jnp.bfloat16)
+        num = jnp.dot(w, value, preferred_element_type=jnp.float32)
+        out_ref[:, cols] = (num[:, :DIM] / num[:, DIM:]).astype(jnp.bfloat16)
+
+
+def self_attention(part, place, q, own, line, across):
+    tokens, width = q.shape
     span = CORES * tokens
     half = KV_HEADS // CORES
     window = (HOPS + 1) * span
@@ -102,24 +104,24 @@
         return [plain] + [pl.BlockSpec((1,) + shape, f) for f in before] + [plain] * HOPS
 
     return pl.pallas_call(
-        self_kernel,
+        functools.partial(self_kernel, part),
         grid_spec=pltpu.PrefetchScalarGridSpec(
             num_scalar_prefetch=1,
             grid=(half,),
-            in_specs=[q_spec, q_spec]
+            in_specs=[q_spec]
             + specs((span, DIM), lambda g: (0, g))
             + specs((span, DIM), lambda g: (0, half + g))
             + specs((ID_ROWS, span), lambda g: (span // ID_ROWS, 0)),
-            out_specs=[q_spec, q_spec],
-            scratch_shapes=[pltpu.VMEM((span, window), jnp.float32)],
+            out_specs=q_spec,
+            scratch_shapes=[pltpu.VMEM((tokens, window), jnp.float32)],
         ),
-        out_shape=[jax.ShapeDtypeStruct((tokens, width), jnp.bfloat16)] * 2,
+        out_shape=jax.ShapeDtypeStruct((tokens, width), jnp.bfloat16),
         compiler_params=pltpu.CompilerParams(vmem_limit_bytes=VMEM),
         cost_estimate=pl.CostEstimate(
-            flops=4 * span * window * width, bytes_accessed=8 * 2**20, transcendentals=span * window * width // DIM
+            flops=4 * tokens * window * width, bytes_accessed=8 * 2**20, transcendentals=tokens * window * width // DIM
         ),
         name="self_attention",
-    )(place, q_own, q_far, *([own] + [line] * HOPS + across) * 3)
+    )(place, q, *([own] + [line] * HOPS + across) * 3)
 
 
 def pick_kernel(rows_ref, places_ref, table_ref, out_ref):
@@ -240,7 +242,8 @@
     images = images.reshape(images.shape[:2] + (-1, DIM))
 
     place = jnp.stack([lax.axis_index("zh"), lax.axis_index("y"), core]).astype(jnp.int32)
-    ctx_own, ctx_other = self_attention(place, q_own, q_far, own, line, [last, back2, back1, back0])
+    ctx_other = self_attention(1, place, q_far, own, line, [last, back2, back1, back0])
+    ctx_own = self_attention(0, place, q_own, own, line, [last, back2, back1, back0])
     ctx_far = move(ctx_other, SWAP)
     mixed = cross_attention(place[2:], jnp.tanh(cross_gate), cq, images, ctx_own, ctx_far)
     return mixed[None]

time: 169 us -> 170 us (level)
  waiting for transfers between devices: 90.4 us -> 84.2 us
  Pallas kernels: 19.1 us -> 24.6 us
    pallas_call x1 -> x2, Pallas kernels: 12.1 us -> 17.6 us  [self_attention(): pl.pallas_call(functools.partial(self_kernel, part), grid_spec=pltpu.Pref...]
    all_to_all x1, waiting for transfers between devices: 7.14 us -> 2.01 us  [on_device(): images = lax.all_to_all(chosen, ('y', 'core'), 0, 0, tiled=True)]
    unnamed x25 -> x23, local copies, waits for them, and re-layouts: 3.16 us -> 3.63 us
  transfers between devices with their start and end apart: 11 -> 11, of which waited for: 8 -> 8; matrix products, arithmetic and copies ran while one was open for 3% -> 3% of each run, Pallas kernels for 9% -> 12%
where the time goes in v3:
time: 170 us; the launch traced here: 169 us
  waiting for transfers between devices  84.2 us (50%)
  starting transfers between devices  36.3 us (21%)
  Pallas kernels  24.6 us (14%)
  between operations  14.3 us (8%)
  local copies, waits for them, and re-layouts  5.84 us (3%)
  other arithmetic  3.87 us (2%)
    ppermute x7, waiting for transfers between devices, move(): return lax.ppermute(value, SEQ, perm)  69.4 us
    pallas_call x2, Pallas kernels, self_attention(): pl.pallas_call(functools.partial(self_kernel, part), grid_spec=pltpu.Pref...  17.6 us
    all_to_all x1, waiting for transfers between devices, on_device(): spread = lax.all_to_all(image, ('y', 'core'), 0, 0, tiled=True)  12.8 us
    ppermute x7, starting transfers between devices, move(): return lax.ppermute(value, SEQ, perm)  11.5 us
    all_to_all x1, starting transfers between devices, on_device(): lax.all_to_all(jnp.concatenate([spread, spread], 0), ('zh',) + DOC, 0, 0,...  9.49 us
    all_to_all x1, starting transfers between devices, on_device(): spread = lax.all_to_all(image, ('y', 'core'), 0, 0, tiled=True)  7.92 us
    all_to_all x1, starting transfers between devices, on_device(): images = lax.all_to_all(chosen, ('y', 'core'), 0, 0, tiled=True)  7.3 us
    pallas_call x1, Pallas kernels, cross_attention(): pl.pallas_call(cross_kernel, grid=(CORES,), in_specs=[smem, smem, q_spec,...  4.51 us
  transfers between devices with their start and end apart: 11, of which 8 were waited for; matrix products, arithmetic and copies ran while one was open for 3% of the time, Pallas kernels for 12%

profile of v3, /device:TPU:257, one launch (start us, length us, event | category | flops | bytes accessed | tf_op | source)
XLA Modules:
  0.0 169.1 jit_solution(12504758305183448157)
XLA Ops:
  6.5 1.1 copy.18
  7.7 0.0 copy-start.6
  7.7 0.9 copy.14
  8.6 7.9 %all-to-all-start = ((bf16[16,16,8,128]{3,2,1,0:T(8,128)(2,1)}), bf16[16,16,8,128]{3,2,1,0:T(8,128)(2,1)S(1)}, u32[]{:S(2)}, u32[]{:S(2)}) async-start(bf16[16,16,8,128]{3,2,1,0:T(8,128)(2,1)} %copy.14), calls=%async_computation | async-start | bytes 1048576 | tf_op jit(solution)/shard_map/all_to_all | solution.py:221
  16.6 0.0 all-gather.3.cloned.1.call-start
  16.6 0.0 copy-done.6
  16.7 0.0 copy-done.8
  16.7 2.0 %collective-permute-start = (bf16[144,1024]{1,0:T(8,128)(2,1)S(1)}, bf16[144,1024]{1,0:T(8,128)(2,1)S(1)}, u32[]{:S(2)}, u32[]{:S(2)}) collective-permute-start(bf16[144,1024]{1,0:T(8,128)(2,1)S(1)} %fusion.1), channel_id=1, source_target_pairs={{0,16},{16,0},{32,48},{48,32},{64,80},{80,64},{96,112},{112,96},{1... | collective-permute-start | bytes 884744 | tf_op jit(solution)/shard_map/ppermute | solution.py:47
  18.7 1.5 collective-permute-done
  20.2 0.9 pad_maximum_fusion.1.refs_0_.refs_9_.refs_18_
  21.1 12.8 %all-to-all-done = bf16[16,16,8,128]{3,2,1,0:T(8,128)(2,1)S(1)} async-done(((bf16[16,16,8,128]{3,2,1,0:T(8,128)(2,1)}), bf16[16,16,8,128]{3,2,1,0:T(8,128)(2,1)S(1)}, u32[]{:S(2)}, u32[]{:S(2)}) %all-to-all-start) | async-done | bytes 524320 | tf_op jit(solution)/shard_map/all_to_all | solution.py:221
  33.9 0.0 all-gather.3.cloned.1.call-update
  33.9 0.1 pad_maximum_fusion
  34.0 1.3 copy.15
  35.2 9.5 %all-to-all-start.1 = ((bf16[32,16,8,128]{3,2,1,0:T(8,128)(2,1)}), bf16[32,16,8,128]{3,2,1,0:T(8,128)(2,1)}, u32[]{:S(2)}, u32[]{:S(2)}) async-start(bf16[32,16,8,128]{3,2,1,0:T(8,128)(2,1)} %copy.15), calls=%async_computation.1 | async-start | bytes 2097152 | tf_op jit(solution)/shard_map/all_to_all | solution.py:228
  44.7 0.0 copy-done
  44.8 1.3 collective-permute-start.1
  46.1 36.3 %collective-permute-done.1.refs_8_.refs_17_.refs_26_ = bf16[272,1024]{1,0:T(8,128)(2,1)S(1)} collective-permute-done((bf16[272,1024]{1,0:T(8,128)(2,1)S(1)}, bf16[272,1024]{1,0:T(8,128)(2,1)S(1)}, u32[]{:S(2)}, u32[]{:S(2)}) %collective-permute-start.1) | collective-permute-done | bytes 557088 | tf_op jit(solution)/shard_map/ppermute | solution.py:47
  82.3 1.3 collective-permute-start.2
  83.6 1.3 collective-permute-start.4
  84.9 19.9 %collective-permute-done.2.refs_7_.refs_16_.refs_25_ = bf16[272,1024]{1,0:T(8,128)(2,1)S(1)} collective-permute-done((bf16[272,1024]{1,0:T(8,128)(2,1)S(1)}, bf16[272,1024]{1,0:T(8,128)(2,1)S(1)}, u32[]{:S(2)}, u32[]{:S(2)}) %collective-permute-start.2) | collective-permute-done | bytes 557088 | tf_op jit(solution)/shard_map/ppermute | solution.py:47
  104.8 1.3 collective-permute-start.3
  106.1 0.0 copy-done.9
  106.1 0.0 copy-done.10
  106.1 0.1 select_reduce_fusion
  106.2 0.7 and_select_fusion
  106.9 0.6 and_select_fusion.1.rows_ref
  107.4 10.3 %collective-permute-done.4.refs_5_.refs_14_.refs_23_ = bf16[272,1024]{1,0:T(8,128)(2,1)S(1)} collective-permute-done((bf16[272,1024]{1,0:T(8,128)(2,1)S(1)}, bf16[272,1024]{1,0:T(8,128)(2,1)S(1)}, u32[]{:S(2)}, u32[]{:S(2)}) %collective-permute-start.4) | collective-permute-done | bytes 557088 | tf_op jit(solution)/shard_map/ppermute | solution.py:47
  117.7 0.8 copy-done.3
  118.6 0.5 collective-permute-done.3.refs_6_.refs_15_.refs_24_
  119.1 0.0 all-to-all-done.1
  119.1 2.5 %pick_images.1 = bf16[32,16,8,128]{3,2,1,0:T(8,128)(2,1)} custom-call(s32[32]{0:T(128)} %and_select_fusion.1.rows_ref, s32[32]{0:T(128)} %get-tuple-element.11.places_ref, bf16[2,16,16,8,128]{4,3,2,1,0:T(8,128)(2,1)} %bitcast.7.table_ref), custom_call_target="tpu_custom_call" | custom-call | bytes 2097152 | tf_op jit(solution)/shard_map/pick_images/pallas_call | solution.py:135
  121.6 0.0 copy-done.1
  121.6 0.0 copy-done.2
  121.6 7.3 %all-to-all-start.2 = ((bf16[16,2,16,8,128]{4,3,2,1,0:T(8,128)(2,1)}), bf16[16,2,16,8,128]{4,3,2,1,0:T(8,128)(2,1)}, u32[]{:S(2)}, u32[]{:S(2)}) async-start(bf16[16,2,16,8,128]{4,3,2,1,0:T(8,128)(2,1)} %bitcast.48), calls=%async_computation.2 | async-start | bytes 2097152 | tf_op jit(solution)/shard_map/all_to_all | solution.py:241
  128.9 0.0 copy-done.4
  128.9 0.9 broadcast_select_fusion
  129.8 2.2 %collective-permute-start.5 = (bf16[128,2048]{1,0:T(8,128)(2,1)S(1)}, bf16[128,2048]{1,0:T(8,128)(2,1)S(1)}, u32[]{:S(2)}, u32[]{:S(2)}) collective-permute-start(bf16[128,2048]{1,0:T(8,128)(2,1)S(1)} %get-tuple-element.13), channel_id=1, source_target_pairs={{0,16},{16,0},{32,48},{48,32},{64,80},{80,64},{96,112},{112,96},{1... | collective-permute-start | bytes 1572872 | tf_op jit(solution)/shard_map/ppermute | solution.py:47
  132.0 0.6 pad_add_fusion.place_ref
  132.6 1.0 collective-permute-done.5.q_ref
  133.6 0.8 copy-done.5
  134.4 8.8 %self_attention.3 = bf16[128,2048]{1,0:T(8,128)(2,1)} custom-call(s32[3]{0:T(128)} %pad_add_fusion.place_ref, bf16[128,2048]{1,0:T(8,128)(2,1)} %copy-done.5, bf16[272,1024]{1,0:T(8,128)(2,1)} %pad_maximum_fusion.1.refs_0_.refs_9_.refs_18_, bf16[8,272,1024]{2,1,0:T(8,128)(2,1)} %bitcast.35, bf16[8,272,1024]{2,1,0:T(8,128)(2,1)} %bitcast.25, ...), custom_call_target="tpu_custom_call" | custom-call | flops 1342177280 | bytes 8388608 | tf_op jit(solution)/shard_map/self_attention/pallas_call | solution.py:106
  143.2 2.2 %collective-permute-start.6 = (bf16[128,2048]{1,0:T(8,128)(2,1)}, bf16[128,2048]{1,0:T(8,128)(2,1)S(1)}, u32[]{:S(2)}, u32[]{:S(2)}) collective-permute-start(bf16[128,2048]{1,0:T(8,128)(2,1)} %self_attention.3), channel_id=1, source_target_pairs={{0,16},{16,0},{32,48},{48,32},{64,80},{80,64},{96,112},{112,96},{1... | collective-permute-start | bytes 1572872 | tf_op jit(solution)/shard_map/ppermute | solution.py:47
  146.1 8.8 %self_attention.2.own_ref = bf16[128,2048]{1,0:T(8,128)(2,1)} custom-call(s32[3]{0:T(128)} %pad_add_fusion.place_ref, bf16[128,2048]{1,0:T(8,128)(2,1)} %get-tuple-element.14.q_ref, bf16[272,1024]{1,0:T(8,128)(2,1)} %pad_maximum_fusion.1.refs_0_.refs_9_.refs_18_, bf16[8,272,1024]{2,1,0:T(8,128)(2,1)} %bitcast.36, bf16[8,272,1024]{2,1,0:T(8,128)(2,1)} %bitcast.37, ...), custom_call_target="tpu_custom_call" | custom-call | flops 1342177280 | bytes 8388608 | tf_op jit(solution)/shard_map/self_attention/pallas_call | solution.py:106
  154.9 2.0 %all-to-all-done.2 = bf16[16,2,16,8,128]{4,3,2,1,0:T(8,128)(2,1)} async-done(((bf16[16,2,16,8,128]{4,3,2,1,0:T(8,128)(2,1)}), bf16[16,2,16,8,128]{4,3,2,1,0:T(8,128)(2,1)}, u32[]{:S(2)}, u32[]{:S(2)}) %all-to-all-start.2) | async-done | bytes 1048608 | tf_op jit(solution)/shard_map/all_to_all | solution.py:241
  157.0 0.0 collective-permute-done.6.far_ref
  157.0 0.8 copy-done.7
  157.7 4.5 %cross_attention.1 = bf16[128,4096]{1,0:T(8,128)(2,1)} custom-call(s32[1]{0:T(128)} %bitcast.core_ref, f32[1]{0:T(128)S(6)} %tanh.3.gate_ref, bf16[128,4096]{1,0:T(8,128)(2,1)} %bitcast.52, bf16[16,2,128,128]{3,2,1,0:T(8,128)(2,1)} %bitcast.9.key_ref.value_ref, bf16[16,2,128,128]{3,2,1,0:T(8,128)(2,1)} %bitcast.9.key_ref.value_ref, ...), custom_call_target="tpu_custom_call" | custom-call | flops 268435456 | bytes 6291456 | tf_op jit(solution)/shard_map/cross_attention/pallas_call | solution.py:175
  (16 shorter events, 0.1 us)
Async XLA Ops:
  7.7 8.9 %copy-start.6 = (bf16[1,128,2048]{2,1,0:T(8,128)(2,1)S(1)}, bf16[1,128,2048]{2,1,0:T(8,128)(2,1)}, u32[]{:S(2)}) copy-start(bf16[1,128,2048]{2,1,0:T(8,128)(2,1)} %param.9) | copy-start | bytes 1572868
  8.6 8.0 %copy-start.8 = (s32[1,128]{1,0:T(1,128)S(1)}, s32[1,128]{1,0:T(1,128)}, u32[]{:S(2)}) copy-start(s32[1,128]{1,0:T(1,128)} %param.10) | copy-start | bytes 1540
  8.6 25.2 %all-to-all-start = ((bf16[16,16,8,128]{3,2,1,0:T(8,128)(2,1)}), bf16[16,16,8,128]{3,2,1,0:T(8,128)(2,1)S(1)}, u32[]{:S(2)}, u32[]{:S(2)}) async-start(bf16[16,16,8,128]{3,2,1,0:T(8,128)(2,1)} %copy.14), calls=%async_computation | async-start | bytes 1048576 | tf_op jit(solution)/shard_map/all_to_all | solution.py:221
  16.6 117.0 %all-gather.3.cloned.1.call-start = ((), (), s32[]{:S(2)}) async-start(), calls=%async_computation.3 | async-start | bytes 5013504 | tf_op jit(solution)/shard_map/all_gather | solution.py:226
  16.7 3.5 %collective-permute-start = (bf16[144,1024]{1,0:T(8,128)(2,1)S(1)}, bf16[144,1024]{1,0:T(8,128)(2,1)S(1)}, u32[]{:S(2)}, u32[]{:S(2)}) collective-permute-start(bf16[144,1024]{1,0:T(8,128)(2,1)S(1)} %fusion.1), channel_id=1, source_target_pairs={{0,16},{16,0},{32,48},{48,32},{64,80},{80,64},{96,112},{112,96},{1... | collective-permute-start | bytes 884744 | tf_op jit(solution)/shard_map/ppermute | solution.py:47
  35.2 9.5 %copy-start = (bf16[272,1024]{1,0:T(8,128)(2,1)S(1)}, bf16[272,1024]{1,0:T(8,128)(2,1)}, u32[]{:S(2)}) copy-start(bf16[272,1024]{1,0:T(8,128)(2,1)} %pad_maximum_fusion.1.refs_0_.refs_9_.refs_18_) | copy-start | bytes 1671172
  35.2 70.8 %copy-start.9 = (s32[1,32]{1,0:T(1,128)S(1)}, s32[1,32]{1,0:T(1,128)}, u32[]{:S(2)}) copy-start(s32[1,32]{1,0:T(1,128)} %param.14) | copy-start | bytes 388
  35.2 70.9 %copy-start.10 = (s32[1,64]{1,0:T(1,128)S(1)}, s32[1,64]{1,0:T(1,128)}, u32[]{:S(2)}) copy-start(s32[1,64]{1,0:T(1,128)} %param.13) | copy-start | bytes 772
  35.2 83.8 %all-to-all-start.1 = ((bf16[32,16,8,128]{3,2,1,0:T(8,128)(2,1)}), bf16[32,16,8,128]{3,2,1,0:T(8,128)(2,1)}, u32[]{:S(2)}, u32[]{:S(2)}) async-start(bf16[32,16,8,128]{3,2,1,0:T(8,128)(2,1)} %copy.15), calls=%async_computation.1 | async-start | bytes 2097152 | tf_op jit(solution)/shard_map/all_to_all | solution.py:228
  44.8 37.6 %collective-permute-start.1 = (bf16[272,1024]{1,0:T(8,128)(2,1)S(1)}, bf16[272,1024]{1,0:T(8,128)(2,1)S(1)}, u32[]{:S(2)}, u32[]{:S(2)}) collective-permute-start(bf16[272,1024]{1,0:T(8,128)(2,1)S(1)} %copy-done), channel_id=1, source_target_pairs={{128,256},{144,272},{160,288},{176,304},{192,320},{208,336},{224,3... | collective-permute-start | bytes 1671176 | tf_op jit(solution)/shard_map/ppermute | solution.py:47
  82.3 39.2 %copy-start.1 = (bf16[272,1024]{1,0:T(8,128)(2,1)}, bf16[272,1024]{1,0:T(8,128)(2,1)S(1)}, u32[]{:S(2)}) copy-start(bf16[272,1024]{1,0:T(8,128)(2,1)S(1)} %collective-permute-done.1.refs_8_.refs_17_.refs_26_) | copy-start | bytes 1671172
  82.3 22.4 %collective-permute-start.2 = (bf16[272,1024]{1,0:T(8,128)(2,1)S(1)}, bf16[272,1024]{1,0:T(8,128)(2,1)S(1)}, u32[]{:S(2)}, u32[]{:S(2)}) collective-permute-start(bf16[272,1024]{1,0:T(8,128)(2,1)S(1)} %collective-permute-done.1.refs_8_.refs_17_.refs_26_), channel_id=1, source_target_pairs={{288,256},{304,272},{320,288},{336,304},{352,320},{368,336},{289,2... | collective-permute-start | bytes 1671176 | tf_op jit(solution)/shard_map/ppermute | solution.py:47
  83.6 34.1 %collective-permute-start.4 = (bf16[272,1024]{1,0:T(8,128)(2,1)S(1)}, bf16[272,1024]{1,0:T(8,128)(2,1)S(1)}, u32[]{:S(2)}, u32[]{:S(2)}) collective-permute-start(bf16[272,1024]{1,0:T(8,128)(2,1)S(1)} %copy-done), channel_id=1, source_target_pairs={{224,256},{240,272},{225,257},{241,273},{226,258},{242,274},{227,2... | collective-permute-start | bytes 1671176 | tf_op jit(solution)/shard_map/ppermute | solution.py:47
  104.8 16.8 %copy-start.2 = (bf16[272,1024]{1,0:T(8,128)(2,1)}, bf16[272,1024]{1,0:T(8,128)(2,1)S(1)}, u32[]{:S(2)}) copy-start(bf16[272,1024]{1,0:T(8,128)(2,1)S(1)} %collective-permute-done.2.refs_7_.refs_16_.refs_25_) | copy-start | bytes 1671172
  104.8 14.3 %collective-permute-start.3 = (bf16[272,1024]{1,0:T(8,128)(2,1)S(1)}, bf16[272,1024]{1,0:T(8,128)(2,1)}, u32[]{:S(2)}, u32[]{:S(2)}) collective-permute-start(bf16[272,1024]{1,0:T(8,128)(2,1)S(1)} %collective-permute-done.2.refs_7_.refs_16_.refs_25_), channel_id=1, source_target_pairs={{288,256},{304,272},{320,288},{336,304},{289,257},{305,273},{321,2... | collective-permute-start | bytes 1671176 | tf_op jit(solution)/shard_map/ppermute | solution.py:47
  117.7 0.9 copy-start.3
  121.6 7.3 %copy-start.4 = (bf16[1,128,4096]{2,1,0:T(8,128)(2,1)S(1)}, bf16[1,128,4096]{2,1,0:T(8,128)(2,1)}, u32[]{:S(2)}) copy-start(bf16[1,128,4096]{2,1,0:T(8,128)(2,1)} %param.8) | copy-start | bytes 3145732
  121.6 35.4 %all-to-all-start.2 = ((bf16[16,2,16,8,128]{4,3,2,1,0:T(8,128)(2,1)}), bf16[16,2,16,8,128]{4,3,2,1,0:T(8,128)(2,1)}, u32[]{:S(2)}, u32[]{:S(2)}) async-start(bf16[16,2,16,8,128]{4,3,2,1,0:T(8,128)(2,1)} %bitcast.48), calls=%async_computation.2 | async-start | bytes 2097152 | tf_op jit(solution)/shard_map/all_to_all | solution.py:241
  129.8 3.8 %collective-permute-start.5 = (bf16[128,2048]{1,0:T(8,128)(2,1)S(1)}, bf16[128,2048]{1,0:T(8,128)(2,1)S(1)}, u32[]{:S(2)}, u32[]{:S(2)}) collective-permute-start(bf16[128,2048]{1,0:T(8,128)(2,1)S(1)} %get-tuple-element.13), channel_id=1, source_target_pairs={{0,16},{16,0},{32,48},{48,32},{64,80},{80,64},{96,112},{112,96},{1... | collective-permute-start | bytes 1572872 | tf_op jit(solution)/shard_map/ppermute | solution.py:47
  133.6 0.8 copy-start.5
  143.2 13.7 %collective-permute-start.6 = (bf16[128,2048]{1,0:T(8,128)(2,1)}, bf16[128,2048]{1,0:T(8,128)(2,1)S(1)}, u32[]{:S(2)}, u32[]{:S(2)}) collective-permute-start(bf16[128,2048]{1,0:T(8,128)(2,1)} %self_attention.3), channel_id=1, source_target_pairs={{0,16},{16,0},{32,48},{48,32},{64,80},{80,64},{96,112},{112,96},{1... | collective-permute-start | bytes 1572872 | tf_op jit(solution)/shard_map/ppermute | solution.py:47
  157.0 0.8 copy-start.7
Sparse Core Ops, SparseCore 0:
  34.0 56.5 all-gather.2
